TPU v7x, 128 devices: a whole 4x4x4 slice. The times are simulated.
128 devices in a mesh: shard: 2 (over core), rep: 64 (over x, z, y).
Axes of the slice: x: 4, y: 4, z: 4, core: 2. Of those that a mesh axis runs over, the one named last changes fastest.
Arguments:
- tokens: bfloat16 [16384, 576], P(('shard', 'rep')), may hold values from -6 to 6
- seq_lengths: int32 [2, 4], P('shard'), may hold values from 1 to 8096, as said below
- attn_gain: bfloat16 [2, 576], P(None, 'shard'), may hold values from 0.5 to 1.5
- w_query: bfloat16 [2, 576, 576], P(None, 'shard'), may hold values from -0.25 to 0.25
- key_weight: bfloat16 [2, 576, 192], P(None, 'shard'), may hold values from -0.25 to 0.25
- value_weight: bfloat16 [2, 576, 192], P(None, 'shard'), may hold values from -0.25 to 0.25
- w_out: bfloat16 [2, 576, 576], P(None, 'shard'), may hold values from -6 to 6
- mlp_gain: bfloat16 [2, 576], P(None, 'shard'), may hold values from 0.5 to 1.5
- w_gate: bfloat16 [2, 576, 1536], P(None, 'shard'), may hold values from -0.25 to 0.25
- w_up: bfloat16 [2, 576, 1536], P(None, 'shard'), may hold values from -0.25 to 0.25
- w_down: bfloat16 [2, 1536, 576], P(None, 'shard'), may hold values from -0.15625 to 0.15625
- cotangent: bfloat16 [16384, 576], P(('shard', 'rep')), may hold values from -6 to 6
Outputs:
- activations: bfloat16 [16384, 576], P(('shard', 'rep'))
- grad_tokens: float32 [16384, 576], P(('shard', 'rep'))
- grad_attn_gain: float32 [2, 576], P(None, 'shard')
- grad_w_query: float32 [2, 576, 576], P(None, 'shard')
- grad_w_key: float32 [2, 576, 192], P(None, 'shard')
- grad_w_value: float32 [2, 576, 192], P(None, 'shard')
- grad_w_out: float32 [2, 576, 576], P(None, 'shard')
- grad_mlp_gain: float32 [2, 576], P(None, 'shard')
- grad_w_gate: float32 [2, 576, 1536], P(None, 'shard')
- grad_w_up: float32 [2, 576, 1536], P(None, 'shard')
- grad_w_down: float32 [2, 1536, 576], P(None, 'shard')
Inputs may be any that keep to these rules, and one draw needn't show every extreme that they name: `seq_lengths`: each pack holds 4 sequences whose lengths sum to 8192; one of them, at a place drawn from the seed, is exactly 8192 - 3 * (32) long, and the others together hold 3 * (32) tokens.
All inputs are finite; a program needn't handle non-finite values.
Results may differ from a plain program's by a relative error of at most 0.03.
Values may be sent and summed in bfloat16 or wider, within the bound.
A program may use at most 256 MiB of HBM per device.

v0:
```python
import math

import jax
import jax.numpy as jnp
from jax import lax
from jax.sharding import PartitionSpec as P

QUERY_HEADS = 9
KEY_VALUE_HEADS = 3
HEAD_SIZE = 64
DECODER_LAYERS = 2


EPSILON = 1e-05


def segment_info(lengths, position_index):
    ends = jnp.cumsum(lengths)
    segment_ids = jnp.sum((position_index[:, None] >= ends[None, :]).astype(jnp.int32), axis=1)
    starts = ends - lengths
    labels = jnp.arange(lengths.shape[0], dtype=jnp.int32)
    first = jnp.sum(jnp.where(segment_ids[:, None] == labels[None, :], starts[None, :], 0), axis=1)
    return (segment_ids, position_index - first)


def rope_tables(position, head_size):
    half = head_size // 2
    freqs = jnp.exp(jnp.arange(half, dtype=jnp.float32) * (-2.0 * math.log(10000.0) / head_size))
    angles = position.astype(jnp.float32)[:, None] * freqs[None, :]
    return (jnp.cos(angles), jnp.sin(angles))


def apply_rotary(value_rows, cosine_table, sine_table):
    half = value_rows.shape[-1] // 2
    first_half = value_rows[..., :half]
    second_half = value_rows[..., half:]
    cosine_table = cosine_table[:, None, :]
    sine_table = sine_table[:, None, :]
    return jnp.concatenate(
        [
            first_half * cosine_table - second_half * sine_table,
            second_half * cosine_table + first_half * sine_table,
        ],
        axis=-1,
    )


def invert_rotary(grads, cosine_table, sine_table):
    half = grads.shape[-1] // 2
    first_half = grads[..., :half]
    second_half = grads[..., half:]
    cosine_table = cosine_table[:, None, :]
    sine_table = sine_table[:, None, :]
    return jnp.concatenate(
        [
            first_half * cosine_table + second_half * sine_table,
            second_half * cosine_table - first_half * sine_table,
        ],
        axis=-1,
    )


def piece_needed(start, token_count, lengths, position_index, segment_mine):
    last_key = jnp.reshape(start + token_count - 1, (1,))
    last_segment = segment_info(lengths, last_key)[0][0]
    return (start <= position_index[-1]) & (last_segment >= segment_mine[0])


def piece_scores(query_rows, key_slice, lengths, position_index, segment_mine):
    token_count = key_slice.shape[0]
    key_index = jnp.arange(token_count, dtype=jnp.int32)
    key_segment = segment_info(lengths, key_index)[0]
    allowed = (key_segment[None, :] == segment_mine[:, None]) & (
        key_index[None, :] <= position_index[:, None]
    )
    scores = jnp.einsum(
        "tkgd,rkd->tkgr",
        query_rows,
        key_slice.reshape(token_count, KEY_VALUE_HEADS, HEAD_SIZE),
        preferred_element_type=jnp.float32,
    )
    return (scores * (1.0 / math.sqrt(HEAD_SIZE)), allowed[:, None, None, :])


def forward_layer(hidden, weights, lengths, position_index, cosine_table, sine_table):
    attn_scale, w_query, key_weight, value_weight, w_out, mlp_scale, w_gate, w_up, w_down = weights
    token_rows = hidden.shape[0]
    query_groups = QUERY_HEADS // KEY_VALUE_HEADS
    inv_one = lax.rsqrt(jnp.mean(hidden * hidden, axis=-1, keepdims=True) + EPSILON)
    normed = (hidden * inv_one * attn_scale.astype(jnp.float32)).astype(jnp.bfloat16)
    query_proj = jnp.dot(normed, w_query, preferred_element_type=jnp.float32)
    projected_keys = jnp.dot(normed, key_weight, preferred_element_type=jnp.float32)
    value_proj = jnp.dot(normed, value_weight, preferred_element_type=jnp.float32)
    query_rows = (
        apply_rotary(
            query_proj.reshape(token_rows, QUERY_HEADS, HEAD_SIZE), cosine_table, sine_table
        )
        .astype(jnp.bfloat16)
        .reshape(token_rows, KEY_VALUE_HEADS, query_groups, HEAD_SIZE)
    )
    keys_now = (
        apply_rotary(
            projected_keys.reshape(token_rows, KEY_VALUE_HEADS, HEAD_SIZE), cosine_table, sine_table
        )
        .astype(jnp.bfloat16)
        .reshape(token_rows, KEY_VALUE_HEADS * HEAD_SIZE)
    )
    values_now = value_proj.astype(jnp.bfloat16)
    segment_mine = segment_info(lengths, position_index)[0]
    start_state = (
        jnp.full((token_rows, KEY_VALUE_HEADS, query_groups), -1e30, jnp.float32),
        jnp.zeros((token_rows, KEY_VALUE_HEADS, query_groups), jnp.float32),
        jnp.zeros((token_rows, KEY_VALUE_HEADS, query_groups, HEAD_SIZE), jnp.float32),
    )
    key_slice = lax.all_gather(keys_now, "rep", axis=0, tiled=True)
    value_slice = lax.all_gather(values_now, "rep", axis=0, tiled=True)
    token_count = key_slice.shape[0]

    def forward_update(state):
        best, total_sum, accum = state
        scores, allowed = piece_scores(query_rows, key_slice, lengths, position_index, segment_mine)
        newbest = jnp.maximum(best, jnp.max(jnp.where(allowed, scores, -1e30), axis=-1))
        expon = jnp.where(allowed, jnp.exp(scores - newbest[..., None]), 0.0)
        total_sum = jnp.sum(expon, axis=-1)
        product = jnp.einsum(
            "tkgr,rkd->tkgd",
            expon.astype(jnp.bfloat16),
            value_slice.reshape(token_count, KEY_VALUE_HEADS, HEAD_SIZE),
            preferred_element_type=jnp.float32,
        )
        return (newbest, total_sum, product)

    needed = piece_needed(jnp.int32(0), token_count, lengths, position_index, segment_mine)
    best, total_sum, accum = lax.cond(needed, forward_update, lambda state: state, start_state)
    attention_output = accum / total_sum[..., None]
    logsum = best + jnp.log(total_sum)
    attended_low = attention_output.reshape(token_rows, QUERY_HEADS * HEAD_SIZE).astype(
        jnp.bfloat16
    )
    middle = hidden + jnp.dot(attended_low, w_out, preferred_element_type=jnp.float32)
    inv_two = lax.rsqrt(jnp.mean(middle * middle, axis=-1, keepdims=True) + EPSILON)
    normed_two = (middle * inv_two * mlp_scale.astype(jnp.float32)).astype(jnp.bfloat16)
    gate = jnp.dot(normed_two, w_gate, preferred_element_type=jnp.float32)
    upward = jnp.dot(normed_two, w_up, preferred_element_type=jnp.float32)
    inner = (jax.nn.silu(gate) * upward).astype(jnp.bfloat16)
    output = middle + jnp.dot(inner, w_down, preferred_element_type=jnp.float32)
    kept = (
        hidden,
        inv_one,
        normed,
        query_rows,
        keys_now,
        values_now,
        attention_output,
        attended_low,
        logsum,
        middle,
        inv_two,
        normed_two,
        gate,
        upward,
        inner,
    )
    return (output, kept)


def backward_layer(grad_out, weights, kept, lengths, position_index, cosine_table, sine_table):
    attn_scale, w_query, key_weight, value_weight, w_out, mlp_scale, w_gate, w_up, w_down = weights
    (
        hidden,
        inv_one,
        normed,
        query_rows,
        keys_now,
        values_now,
        attention_output,
        attended_low,
        logsum,
        middle,
        inv_two,
        normed_two,
        gate,
        upward,
        inner,
    ) = kept
    token_rows = hidden.shape[0]
    query_groups = QUERY_HEADS // KEY_VALUE_HEADS
    feature_width = KEY_VALUE_HEADS * HEAD_SIZE
    grad_branch = grad_out.astype(jnp.bfloat16)
    grad_down = jnp.einsum("tf,td->fd", inner, grad_branch, preferred_element_type=jnp.float32)
    grad_inner = jnp.einsum("td,fd->tf", grad_branch, w_down, preferred_element_type=jnp.float32)
    sigma = jax.nn.sigmoid(gate)
    grad_gate = (grad_inner * upward * sigma * (1.0 + gate * (1.0 - sigma))).astype(jnp.bfloat16)
    grad_upward = (grad_inner * gate * sigma).astype(jnp.bfloat16)
    grad_gate_weight = jnp.einsum(
        "tc,tf->cf", normed_two, grad_gate, preferred_element_type=jnp.float32
    )
    grad_up_weight = jnp.einsum(
        "tc,tf->cf", normed_two, grad_upward, preferred_element_type=jnp.float32
    )
    grad_normed_two = jnp.einsum(
        "tf,cf->tc", grad_gate, w_gate, preferred_element_type=jnp.float32
    ) + jnp.einsum("tf,cf->tc", grad_upward, w_up, preferred_element_type=jnp.float32)
    grad_mlp_scale = jnp.sum(middle * inv_two * grad_normed_two, axis=0)
    scaled_two = grad_normed_two * mlp_scale.astype(jnp.float32)
    grad_middle = (
        grad_out
        + inv_two * scaled_two
        - middle * inv_two**3 * jnp.mean(scaled_two * middle, axis=-1, keepdims=True)
    )
    grad_attn_branch = grad_middle.astype(jnp.bfloat16)
    grad_out_weight = jnp.einsum(
        "th,td->hd", attended_low, grad_attn_branch, preferred_element_type=jnp.float32
    )
    grad_attended = (
        jnp.einsum("td,hd->th", grad_attn_branch, w_out, preferred_element_type=jnp.float32)
        .astype(jnp.bfloat16)
        .reshape(token_rows, KEY_VALUE_HEADS, query_groups, HEAD_SIZE)
    )
    delta = jnp.sum(grad_attended.astype(jnp.float32) * attention_output, axis=-1)
    segment_mine = segment_info(lengths, position_index)[0]
    pack_rows = token_rows * lax.axis_size("rep")
    scale = 1.0 / math.sqrt(HEAD_SIZE)
    start_state = (
        jnp.zeros((token_rows, KEY_VALUE_HEADS, query_groups, HEAD_SIZE), jnp.float32),
        jnp.zeros((pack_rows, 2 * feature_width), jnp.float32),
    )
    key_slice = lax.all_gather(keys_now, "rep", axis=0, tiled=True)
    value_slice = lax.all_gather(values_now, "rep", axis=0, tiled=True)
    token_count = key_slice.shape[0]

    def backward_update(state):
        scores, allowed = piece_scores(query_rows, key_slice, lengths, position_index, segment_mine)
        weights_blk = jnp.where(allowed, jnp.exp(scores - logsum[..., None]), 0.0)
        grad_weights = jnp.einsum(
            "tkgd,rkd->tkgr",
            grad_attended,
            value_slice.reshape(token_count, KEY_VALUE_HEADS, HEAD_SIZE),
            preferred_element_type=jnp.float32,
        )
        grad_scores = (weights_blk * (grad_weights - delta[..., None]) * scale).astype(jnp.bfloat16)
        grad_queries = jnp.einsum(
            "tkgr,rkd->tkgd",
            grad_scores,
            key_slice.reshape(token_count, KEY_VALUE_HEADS, HEAD_SIZE),
            preferred_element_type=jnp.float32,
        )
        grad_keys = jnp.einsum(
            "tkgr,tkgd->rkd", grad_scores, query_rows, preferred_element_type=jnp.float32
        )
        grad_values = jnp.einsum(
            "tkgr,tkgd->rkd",
            weights_blk.astype(jnp.bfloat16),
            grad_attended,
            preferred_element_type=jnp.float32,
        )
        joined = jnp.concatenate(
            [
                grad_keys.reshape(token_count, feature_width),
                grad_values.reshape(token_count, feature_width),
            ],
            axis=1,
        )
        return (grad_queries, joined)

    needed = piece_needed(jnp.int32(0), token_count, lengths, position_index, segment_mine)
    grad_queries, buffer = lax.cond(needed, backward_update, lambda state: state, start_state)
    key_value_gradient = lax.psum_scatter(buffer, "rep", scatter_dimension=0, tiled=True)
    grad_key_proj = (
        invert_rotary(
            key_value_gradient[:, :feature_width].reshape(token_rows, KEY_VALUE_HEADS, HEAD_SIZE),
            cosine_table,
            sine_table,
        )
        .reshape(token_rows, feature_width)
        .astype(jnp.bfloat16)
    )
    grad_value_proj = key_value_gradient[:, feature_width:].astype(jnp.bfloat16)
    grad_query_proj = (
        invert_rotary(
            grad_queries.reshape(token_rows, QUERY_HEADS, HEAD_SIZE), cosine_table, sine_table
        )
        .reshape(token_rows, QUERY_HEADS * HEAD_SIZE)
        .astype(jnp.bfloat16)
    )
    grad_query_weight = jnp.einsum(
        "tc,th->ch", normed, grad_query_proj, preferred_element_type=jnp.float32
    )
    grad_key_weight = jnp.einsum(
        "tc,th->ch", normed, grad_key_proj, preferred_element_type=jnp.float32
    )
    grad_value_weight = jnp.einsum(
        "tc,th->ch", normed, grad_value_proj, preferred_element_type=jnp.float32
    )
    grad_normed = jnp.einsum(
        "th,ch->tc", grad_query_proj, w_query, preferred_element_type=jnp.float32
    )
    grad_normed = grad_normed + jnp.einsum(
        "th,ch->tc", grad_key_proj, key_weight, preferred_element_type=jnp.float32
    )
    grad_normed = grad_normed + jnp.einsum(
        "th,ch->tc", grad_value_proj, value_weight, preferred_element_type=jnp.float32
    )
    grad_attn_scale = jnp.sum(hidden * inv_one * grad_normed, axis=0)
    scaled_one = grad_normed * attn_scale.astype(jnp.float32)
    grad_input = (
        grad_middle
        + inv_one * scaled_one
        - hidden * inv_one**3 * jnp.mean(scaled_one * hidden, axis=-1, keepdims=True)
    )
    layer_grads = (
        grad_attn_scale,
        grad_query_weight,
        grad_key_weight,
        grad_value_weight,
        grad_out_weight,
        grad_mlp_scale,
        grad_gate_weight,
        grad_up_weight,
        grad_down,
    )
    return (grad_input, layer_grads)


def per_device(
    tokens,
    seq_lengths,
    attn_gain,
    w_query,
    key_weight,
    value_weight,
    w_out,
    mlp_gain,
    w_gate,
    w_up,
    w_down,
    cotangent,
):
    token_rows = tokens.shape[0]
    lengths = seq_lengths[0]
    position_index = lax.axis_index("rep") * token_rows + jnp.arange(token_rows, dtype=jnp.int32)
    position = segment_info(lengths, position_index)[1]
    cosine_table, sine_table = rope_tables(position, HEAD_SIZE)
    hidden = tokens.astype(jnp.float32)
    kept_layers = []
    gathered_layers = []
    for layer_no in range(DECODER_LAYERS):
        weights = (
            lax.all_gather(attn_gain[layer_no], "shard", axis=0, tiled=True),
            lax.all_gather(w_query[layer_no], "shard", axis=0, tiled=True),
            lax.all_gather(key_weight[layer_no], "shard", axis=0, tiled=True),
            lax.all_gather(value_weight[layer_no], "shard", axis=0, tiled=True),
            lax.all_gather(w_out[layer_no], "shard", axis=0, tiled=True),
            lax.all_gather(mlp_gain[layer_no], "shard", axis=0, tiled=True),
            lax.all_gather(w_gate[layer_no], "shard", axis=0, tiled=True),
            lax.all_gather(w_up[layer_no], "shard", axis=0, tiled=True),
            lax.all_gather(w_down[layer_no], "shard", axis=0, tiled=True),
        )
        hidden, kept = forward_layer(
            hidden, weights, lengths, position_index, cosine_table, sine_table
        )
        kept_layers.append(kept)
        gathered_layers.append(weights)
    activations = hidden.astype(jnp.bfloat16)
    grad = cotangent.astype(jnp.float32)
    collected = [None] * DECODER_LAYERS
    for layer_no in reversed(range(DECODER_LAYERS)):
        weights = (
            lax.all_gather(attn_gain[layer_no], "shard", axis=0, tiled=True),
            lax.all_gather(w_query[layer_no], "shard", axis=0, tiled=True),
            lax.all_gather(key_weight[layer_no], "shard", axis=0, tiled=True),
            lax.all_gather(value_weight[layer_no], "shard", axis=0, tiled=True),
            lax.all_gather(w_out[layer_no], "shard", axis=0, tiled=True),
            lax.all_gather(mlp_gain[layer_no], "shard", axis=0, tiled=True),
            lax.all_gather(w_gate[layer_no], "shard", axis=0, tiled=True),
            lax.all_gather(w_up[layer_no], "shard", axis=0, tiled=True),
            lax.all_gather(w_down[layer_no], "shard", axis=0, tiled=True),
        )
        grad, layer_grads = backward_layer(
            grad, weights, kept_layers[layer_no], lengths, position_index, cosine_table, sine_table
        )
        owned = (
            lax.psum_scatter(
                layer_grads[0].astype(jnp.bfloat16), "shard", scatter_dimension=0, tiled=True
            ).astype(jnp.float32),
            lax.psum_scatter(
                layer_grads[1].astype(jnp.bfloat16), "shard", scatter_dimension=0, tiled=True
            ).astype(jnp.float32),
            lax.psum_scatter(
                layer_grads[2].astype(jnp.bfloat16), "shard", scatter_dimension=0, tiled=True
            ).astype(jnp.float32),
            lax.psum_scatter(
                layer_grads[3].astype(jnp.bfloat16), "shard", scatter_dimension=0, tiled=True
            ).astype(jnp.float32),
            lax.psum_scatter(
                layer_grads[4].astype(jnp.bfloat16), "shard", scatter_dimension=0, tiled=True
            ).astype(jnp.float32),
            lax.psum_scatter(
                layer_grads[5].astype(jnp.bfloat16), "shard", scatter_dimension=0, tiled=True
            ).astype(jnp.float32),
            lax.psum_scatter(
                layer_grads[6].astype(jnp.bfloat16), "shard", scatter_dimension=0, tiled=True
            ).astype(jnp.float32),
            lax.psum_scatter(
                layer_grads[7].astype(jnp.bfloat16), "shard", scatter_dimension=0, tiled=True
            ).astype(jnp.float32),
            lax.psum_scatter(
                layer_grads[8].astype(jnp.bfloat16), "shard", scatter_dimension=0, tiled=True
            ).astype(jnp.float32),
        )
        owned = lax.psum(
            (
                owned[0],
                owned[1],
                owned[2],
                owned[3],
                owned[4],
                owned[5],
                owned[6],
                owned[7],
                owned[8],
            ),
            "rep",
        )
        collected[layer_no] = owned
    stacked = [
        jnp.stack([collected[layer_no][member] for layer_no in range(DECODER_LAYERS)])
        for member in range(9)
    ]
    return (
        activations,
        grad,
        stacked[0],
        stacked[1],
        stacked[2],
        stacked[3],
        stacked[4],
        stacked[5],
        stacked[6],
        stacked[7],
        stacked[8],
    )


def solution(mesh):
    placed = (
        P(("shard", "rep"), None),
        P("shard", None),
        P(None, "shard"),
        P(None, "shard", None),
        P(None, "shard", None),
        P(None, "shard", None),
        P(None, "shard", None),
        P(None, "shard"),
        P(None, "shard", None),
        P(None, "shard", None),
        P(None, "shard", None),
        P(("shard", "rep"), None),
    )
    return jax.shard_map(
        per_device,
        mesh=mesh,
        in_specs=placed,
        out_specs=(
            P(("shard", "rep"), None),
            P(("shard", "rep"), None),
            P(None, "shard"),
            P(None, "shard", None),
            P(None, "shard", None),
            P(None, "shard", None),
            P(None, "shard", None),
            P(None, "shard"),
            P(None, "shard", None),
            P(None, "shard", None),
            P(None, "shard", None),
        ),
        check_vma=False,
    )
```

profile of v0, /device:TPU:1, one launch (start us, length us, event | category | flops | bytes accessed | tf_op | source)
XLA Modules:
  0.0 1492.9 jit_solution(7970096890011104579)
XLA Ops:
  10.5 3.1 all-gather.1
  18.0 2.5 all-reduce.11
  31.6 2.9 fusion.141
  38.6 2.3 all-gather.2
  43.6 2.3 all-gather.4
  48.7 49.3 %all-gather.29.cloned.1.call-done = bf16[8192,192]{0,1:T(8,128)(2,1)} async-done(((bf16[128,192]{0,1:T(8,128)(2,1)}), bf16[8192,192]{0,1:T(8,128)(2,1)}) %all-gather.29.cloned.1.call-update) | async-done | bytes 3145744 | tf_op jit(solution)/shard_map/all_gather | solution.py:115
  98.0 74.7 %all-gather.31.cloned.1.call-done = bf16[8192,192]{0,1:T(8,128)(2,1)} async-done(((bf16[128,192]{0,1:T(8,128)(2,1)}), bf16[8192,192]{0,1:T(8,128)(2,1)}) %all-gather.31.cloned.1.call-update) | async-done | bytes 3145744 | tf_op jit(solution)/shard_map/all_gather | solution.py:116
  172.8 56.5 %conditional.4 = (f32[128,3,3]{0,2,1:T(4,128)}, f32[128,3,3]{0,2,1:T(4,128)}, f32[128,3,3,64]{0,3,2,1:T(8,128)S(1)}, f32[128,3,3]{0,2,1:T(4,128)S(1)}) conditional(s32[]{:T(128)} %convert_element_type.320, () %tuple.62, (s32[4]{0:T(128)S(1)}, s32[128]{0:T(128)S(1)}, s32[128]{0:T(128)S(1)}, bf16[8192,192]{0,1:T(8,128)(2,1)}, ...), branch_computations={%region_5.6_spmd, %region_6.11_spmd} | conditional | flops 2522962944 | bytes 124277840 | solution.py:134
  173.4 3.7 fusion.8
  177.1 17.2 %fusion = (f32[128,3,3]{0,2,1:T(4,128)S(1)}, f32[3,8192,128,3]{2,1,3,0:T(8,128)}) fusion(pred[128,8192]{0,1:T(8,128)(4,1)S(1)} %fusion.8, bf16[8192,3,64,1]{0,2,3,1:T(8,128)(2,1)} %bitcast.393, bf16[128,3,3,64]{0,3,2,1:T(8,128)(2,1)} %get-tuple-element.170), kind=kOutput, calls=%fused_computation.2 | convolution fusion | flops 1236269952 | bytes 42095104 | tf_op jit(solution)/shard_map/cond/branch_1_fun/tkgd,rkd->tkgr/dot_general | solution.py:76
  194.9 16.9 %fusion.4 = f32[128,3,3]{0,2,1:T(4,128)} fusion(f32[3,8192,128,3]{2,1,3,0:T(8,128)} %get-tuple-element.300, f32[128,3,3]{0,2,1:T(4,128)} %broadcast_maximum_fusion, pred[128,8192]{0,1:T(8,128)(4,1)S(1)} %fusion.8), kind=kLoop, calls=%fused_computation.6 | loop fusion | flops 37747584 | bytes 38806528 | tf_op jit(solution)/shard_map/cond/branch_1_fun/reduce_sum | solution.py:124
  211.8 16.7 %fusion.9 = f32[128,3,3,64]{0,3,2,1:T(8,128)S(1)} fusion(bf16[8192,3,64,1]{0,2,3,1:T(8,128)(2,1)} %bitcast.444, f32[3,8192,128,3]{2,1,3,0:T(8,128)} %get-tuple-element.300, f32[128,3,3]{0,2,1:T(4,128)} %broadcast_maximum_fusion, pred[128,8192]{0,1:T(8,128)(4,1)S(1)} %fusion.8), kind=kOutput, calls=%fused_computation.11 | convolution fusion | flops 1245708288 | bytes 42242560 | tf_op jit(solution)/shard_map/cond/branch_1_fun/tkgr,rkd->tkgd/dot_general | solution.py:125
  234.1 3.3 multiply_convert_fusion.5
  237.4 2.3 multiply_reduce_fusion.9
  240.9 3.1 all-gather.12
  246.3 2.3 all-gather.11
  248.7 2.3 all-gather.13
  251.0 3.1 fusion.52
  255.3 57.0 %all-gather.33.cloned.1.call-done = bf16[8192,192]{0,1:T(8,128)(2,1)} async-done(((bf16[128,192]{0,1:T(8,128)(2,1)}), bf16[8192,192]{0,1:T(8,128)(2,1)}) %all-gather.33.cloned.1.call-update) | async-done | bytes 3145744 | tf_op jit(solution)/shard_map/all_gather | solution.py:115
  312.4 74.7 %all-gather.35.cloned.1.call-done = bf16[8192,192]{0,1:T(8,128)(2,1)} async-done(((bf16[128,192]{0,1:T(8,128)(2,1)}), bf16[8192,192]{0,1:T(8,128)(2,1)}) %all-gather.35.cloned.1.call-update) | async-done | bytes 3145744 | tf_op jit(solution)/shard_map/all_gather | solution.py:116
  387.1 56.0 %conditional.5 = (f32[128,3,3]{0,2,1:T(4,128)}, f32[128,3,3]{0,2,1:T(4,128)}, f32[128,3,3,64]{0,3,2,1:T(8,128)S(1)}, f32[128,3,3]{0,2,1:T(4,128)S(1)}) conditional(s32[]{:T(128)} %convert_element_type.320, () %tuple.64, (s32[4]{0:T(128)S(1)}, s32[128]{0:T(128)S(1)}, s32[128]{0:T(128)S(1)}, bf16[8192,192]{0,1:T(8,128)(2,1)}, ...), branch_computations={%region_13.14_spmd, %region_14.19_spmd} | conditional | flops 2522962944 | bytes 124277840 | solution.py:134
  388.0 3.7 fusion.22
  391.8 17.2 %fusion.14 = (f32[128,3,3]{0,2,1:T(4,128)S(1)}, f32[3,8192,128,3]{2,1,3,0:T(8,128)}) fusion(pred[128,8192]{0,1:T(8,128)(4,1)S(1)} %fusion.22, bf16[8192,3,64,1]{0,2,3,1:T(8,128)(2,1)} %bitcast.396, bf16[128,3,3,64]{0,3,2,1:T(8,128)(2,1)} %get-tuple-element.176), kind=kOutput, calls=%fused_computation.19 | convolution fusion | flops 1236269952 | bytes 42095104 | tf_op jit(solution)/shard_map/cond/branch_1_fun/tkgd,rkd->tkgr/dot_general | solution.py:76
  409.6 16.9 %fusion.18 = f32[128,3,3]{0,2,1:T(4,128)} fusion(f32[3,8192,128,3]{2,1,3,0:T(8,128)} %get-tuple-element.302, f32[128,3,3]{0,2,1:T(4,128)} %broadcast_maximum_fusion.1, pred[128,8192]{0,1:T(8,128)(4,1)S(1)} %fusion.22), kind=kLoop, calls=%fused_computation.23 | loop fusion | flops 37747584 | bytes 38806528 | tf_op jit(solution)/shard_map/cond/branch_1_fun/reduce_sum | solution.py:124
  426.5 15.9 %fusion.23 = f32[128,3,3,64]{0,3,2,1:T(8,128)S(1)} fusion(bf16[8192,3,64,1]{0,2,3,1:T(8,128)(2,1)} %bitcast.446, f32[3,8192,128,3]{2,1,3,0:T(8,128)} %get-tuple-element.302, f32[128,3,3]{0,2,1:T(4,128)} %broadcast_maximum_fusion.1, pred[128,8192]{0,1:T(8,128)(4,1)S(1)} %fusion.22), kind=kOutput, calls=%fused_computation.28 | convolution fusion | flops 1245708288 | bytes 42242560 | tf_op jit(solution)/shard_map/cond/branch_1_fun/tkgr,rkd->tkgd/dot_general | solution.py:125
  448.2 3.2 multiply_convert_fusion.3
  454.5 96.0 %conditional.6 = (f32[8192,384]{0,1:T(8,128)}, f32[128,9,32]{0,2,1:T(8,128)}, f32[128,9,32]{0,2,1:T(8,128)}) conditional(s32[]{:T(128)} %convert_element_type.320, () %tuple.66, (s32[4]{0:T(128)S(1)}, s32[128]{0:T(128)S(1)}, s32[128]{0:T(128)S(1)}, bf16[8192,192]{0,1:T(8,128)(2,1)S(1)}, bf16[128,3,3,64]{0,3,2,1:T(8,128)(2,1)}, ...), branch_computations={%region_21.22_spmd, %region_22.26_spmd} | conditional | flops 6150209536 | bytes 227590784 | solution.py:267
  454.7 15.6 %fusion.147 = f32[3,8192,128,3]{2,1,3,0:T(8,128)} fusion(bf16[8192,3,64,1]{0,2,3,1:T(8,128)(2,1)S(1)} %bitcast.397, bf16[128,3,3,64]{0,3,2,1:T(8,128)(2,1)} %get-tuple-element.182), kind=kOutput, calls=%fused_computation.281 | convolution fusion | flops 1207959552 | bytes 41041920 | tf_op jit(solution)/shard_map/cond/branch_1_fun/tkgd,rkd->tkgr/dot_general | solution.py:76
  471.4 3.7 fusion.37
  475.2 17.5 %fusion.34 = f32[3,8192,64,1]{1,2,3,0:T(8,128)} fusion(bf16[128,3,3,64]{0,3,2,1:T(8,128)(2,1)} %bitcast.29, f32[3,8192,128,3]{2,1,3,0:T(8,128)} %fusion.147, f32[128,3,3]{0,2,1:T(4,128)S(1)} %add.192, pred[128,8192]{0,1:T(8,128)(4,1)S(1)} %fusion.37), kind=kOutput, calls=%fused_computation.42 | convolution fusion | flops 1245708288 | bytes 45240832 | tf_op jit(solution)/shard_map/cond/branch_1_fun/tkgr,tkgd->rkd/dot_general | solution.py:251
  493.6 25.9 %fusion.30 = bf16[128,3,3,8192]{0,3,2,1:T(8,128)(2,1)} fusion(f32[3,8192,128,3]{2,1,3,0:T(8,128)} %fusion.147, f32[128,3,3]{0,2,1:T(4,128)S(1)} %multiply_reduce_fusion, f32[128,3,3]{0,2,1:T(4,128)S(1)} %add.192, pred[128,8192]{0,1:T(8,128)(4,1)} %copy-done.67, bf16[8192,3,64,1]{0,2,3,1:T(8,128)(2,1)} %bitcast.447, bf16[128,3,3,64]{0,3,2,1:T(8,128)(2,1)} %bitcast.29), kind=kOutput, calls=%fused_computation.37 | convolution fusion | flops 1274019840 | bytes 60974080 | tf_op jit(solution)/shard_map/cond/branch_1_fun/tkgd,rkd->tkgr/dot_general | solution.py:235
  519.5 11.6 fusion.148
  531.1 10.6 pad_maximum_fusion
  541.7 7.9 fusion.149
  560.7 218.7 %reduce-scatter.17.cloned.1.call-done = f32[128,384]{0,1:T(8,128)} async-done(((f32[8192,384]{0,1:T(8,128)}), f32[128,384]{0,1:T(8,128)}) %reduce-scatter.17.cloned.1.call-update) | async-done | bytes 196624 | tf_op jit(solution)/shard_map/reduce_scatter | solution.py:268
  782.1 2.7 multiply_convert_fusion.1
  789.2 2.3 convolution_convert_fusion.14
  791.5 97.4 %conditional.7 = (f32[8192,384]{0,1:T(8,128)}, f32[128,9,32]{0,2,1:T(8,128)}, f32[128,9,32]{0,2,1:T(8,128)}) conditional(s32[]{:T(128)} %convert_element_type.320, () %tuple.68, (s32[4]{0:T(128)S(1)}, s32[128]{0:T(128)S(1)}, s32[128]{0:T(128)S(1)}, bf16[8192,192]{0,1:T(8,128)(2,1)S(1)}, bf16[128,3,3,64]{0,3,2,1:T(8,128)(2,1)}, ...), branch_computations={%region_29.30_spmd, %region_30.34_spmd} | conditional | flops 6150209536 | bytes 227590784 | solution.py:267
  792.0 16.0 %fusion.150 = f32[3,8192,128,3]{2,1,3,0:T(8,128)} fusion(bf16[8192,3,64,1]{0,2,3,1:T(8,128)(2,1)S(1)} %bitcast.394, bf16[128,3,3,64]{0,3,2,1:T(8,128)(2,1)} %get-tuple-element.192), kind=kOutput, calls=%fused_computation.284 | convolution fusion | flops 1207959552 | bytes 41041920 | tf_op jit(solution)/shard_map/cond/branch_1_fun/tkgd,rkd->tkgr/dot_general | solution.py:76
  809.0 3.7 fusion.49
  812.8 17.8 %fusion.46 = f32[3,8192,64,1]{1,2,3,0:T(8,128)} fusion(bf16[128,3,3,64]{0,3,2,1:T(8,128)(2,1)} %bitcast.53, f32[3,8192,128,3]{2,1,3,0:T(8,128)} %fusion.150, f32[128,3,3]{0,2,1:T(4,128)S(1)} %add.193, pred[128,8192]{0,1:T(8,128)(4,1)S(1)} %fusion.49), kind=kOutput, calls=%fused_computation.60 | convolution fusion | flops 1245708288 | bytes 45240832 | tf_op jit(solution)/shard_map/cond/branch_1_fun/tkgr,tkgd->rkd/dot_general | solution.py:251
  831.5 26.4 %fusion.42 = bf16[128,3,3,8192]{0,3,2,1:T(8,128)(2,1)} fusion(f32[3,8192,128,3]{2,1,3,0:T(8,128)} %fusion.150, f32[128,3,3]{0,2,1:T(4,128)S(1)} %multiply_reduce_fusion.1, f32[128,3,3]{0,2,1:T(4,128)S(1)} %add.193, pred[128,8192]{0,1:T(8,128)(4,1)} %copy-done.68, bf16[8192,3,64,1]{0,2,3,1:T(8,128)(2,1)} %bitcast.445, bf16[128,3,3,64]{0,3,2,1:T(8,128)(2,1)} %bitcast.53), kind=kOutput, calls=%fused_computation.55 | convolution fusion | flops 1274019840 | bytes 60974080 | tf_op jit(solution)/shard_map/cond/branch_1_fun/tkgd,rkd->tkgr/dot_general | solution.py:235
  857.9 11.6 fusion.151
  869.5 10.6 pad_maximum_fusion.1
  880.1 7.9 fusion.152
  906.3 2.5 bitcast_convert_fusion
  908.8 2.6 bitcast_convert_fusion.4
  911.4 2.6 bitcast_convert_fusion.2
  919.2 11.5 reduce-scatter.33.cloned.1.call-done
  932.6 14.5 reduce-scatter.37.cloned.1.call-done
  947.0 2.6 bitcast_convert_fusion.5
  949.6 231.4 %reduce-scatter.19.cloned.1.call-done = f32[128,384]{0,1:T(8,128)} async-done(((f32[8192,384]{0,1:T(8,128)}), f32[128,384]{0,1:T(8,128)}) %reduce-scatter.19.cloned.1.call-update) | async-done | bytes 196624 | tf_op jit(solution)/shard_map/reduce_scatter | solution.py:268
  1183.0 12.0 reduce-scatter.41.cloned.1.call-done
  1195.0 2.6 bitcast_convert_fusion.3
  1199.6 11.1 reduce-scatter.45.cloned.1.call-done
  1210.7 2.5 bitcast_convert_fusion.1
  1213.2 12.2 reduce-scatter.25.cloned.1.call-done
  1227.1 12.3 reduce-scatter.29.cloned.1.call-done
  1242.7 2.3 fusion.88
  1246.9 2.5 all-reduce.10
  1249.6 156.1 %all-reduce.8 = (f32[1,288]{1,0:T(1,128)S(1)}, f32[1,288]{1,0:T(1,128)S(1)}, f32[1,288]{1,0:T(1,128)S(1)}, f32[1,288]{1,0:T(1,128)S(1)}) all-reduce(f32[1,288]{1,0:T(1,128)S(1)} %stack.82, f32[1,288]{1,0:T(1,128)S(1)} %stack.81, f32[1,288]{1,0:T(1,128)S(1)} %stack.97, ...), channel_id=1, replica_groups=mesh['shard'=2,'rep'=64] {'rep'}, use_global_device_ids=true, to_apply=%region_41.42 | all-reduce | flops 1152 | bytes 9216 | tf_op jit(solution)/shard_map/psum | solution.py:411
  1407.7 65.7 %all-reduce.14.cloned.1.call-done = (f32[1,288,576]{2,1,0:T(8,128)}, f32[1,288,576]{2,1,0:T(8,128)}, f32[1,288,192]{2,1,0:T(8,128)}, f32[1,288,192]{2,1,0:T(8,12...) async-done(((f32[1,288,576]{2,1,0:T(8,128)}, ...) | async-done | bytes 14155792 | tf_op jit(solution)/shard_map/psum | solution.py:411
  1473.5 4.2 pad_maximum_fusion.4
  1482.2 3.7 pad_maximum_fusion.2
  (391 shorter events, 110.1 us)
Async XLA Ops:
  7.2 23.0 %copy-start.38 = (bf16[2,288,1536]{2,1,0:T(8,128)(2,1)S(1)}, bf16[2,288,1536]{2,1,0:T(8,128)(2,1)}, u32[]{:S(2)}) copy-start(bf16[2,288,1536]{2,1,0:T(8,128)(2,1)} %param.28) | copy-start | bytes 5308420
  7.2 90.8 %all-gather.29.cloned.1.call-start = ((), (), s32[]{:S(2)}) async-start(), calls=%async_computation.16 | async-start | bytes 3194880 | tf_op jit(solution)/shard_map/all_gather | solution.py:115
  13.6 20.9 %copy-start.29 = (bf16[1,576,192]{2,1,0:T(8,128)(2,1)}, bf16[1,576,192]{2,1,0:T(8,128)(2,1)S(1)}, u32[]{:S(2)}) copy-start(bf16[1,576,192]{2,1,0:T(8,128)(2,1)S(1)} %all-gather.1) | copy-start | bytes 663556
  20.5 20.4 %copy-start.82 = (f32[576]{0:T(1024)}, f32[576]{0:T(1024)S(1)}, u32[]{:S(2)}) copy-start(f32[576]{0:T(1024)S(1)} %convert_element_type.395) | copy-start | bytes 6916
  22.1 18.8 %copy-start.84 = (f32[128]{0:T(128)}, f32[128]{0:T(128)S(1)}, u32[]{:S(2)}) copy-start(f32[128]{0:T(128)S(1)} %get-tuple-element.347) | copy-start | bytes 1540
  24.4 148.4 %all-gather.31.cloned.1.call-start = ((), (), s32[]{:S(2)}) async-start(), calls=%async_computation.17 | async-start | bytes 3194880 | tf_op jit(solution)/shard_map/all_gather | solution.py:116
  30.2 201.8 %all-gather.37.cloned.1.call-start = ((), (), s32[]{:S(2)}) async-start(), calls=%async_computation.36 | async-start | bytes 2654208 | tf_op jit(solution)/shard_map/all_gather | solution.py:355
  31.6 6.9 copy-start.71
  31.6 202.5 %all-gather.39.cloned.1.call-start = ((), (), s32[]{:S(2)}) async-start(), calls=%async_computation.37 | async-start | bytes 2654208 | tf_op jit(solution)/shard_map/all_gather | solution.py:356
  34.5 7.2 copy-start.2
  34.6 202.9 %all-gather.41.cloned.1.call-start = ((), (), s32[]{:S(2)}) async-start(), calls=%async_computation.38 | async-start | bytes 2654208 | tf_op jit(solution)/shard_map/all_gather | solution.py:357
  36.0 215.0 %all-gather.47.cloned.1.call-start = ((), (), s32[]{:S(2)}) async-start(), calls=%async_computation.41 | async-start | bytes 2654208 | tf_op jit(solution)/shard_map/all_gather | solution.py:357
  36.0 136.7 %copy-start.91 = (s32[1,4]{1,0:T(1,128)S(1)}, s32[1,4]{1,0:T(1,128)}, u32[]{:S(2)}) copy-start(s32[1,4]{1,0:T(1,128)} %param.21) | copy-start | bytes 52
  36.5 275.8 %all-gather.33.cloned.1.call-start = ((), (), s32[]{:S(2)}) async-start(), calls=%async_computation.18 | async-start | bytes 3194880 | tf_op jit(solution)/shard_map/all_gather | solution.py:115
  45.9 184.8 %copy-start.16 = (bf16[1,576,576]{2,1,0:T(8,128)(2,1)}, bf16[1,576,576]{2,1,0:T(8,128)(2,1)S(1)}, u32[]{:S(2)}) copy-start(bf16[1,576,576]{2,1,0:T(8,128)(2,1)S(1)} %all-gather.4) | copy-start | bytes 1990660
  47.9 191.9 %copy-start.30 = (bf16[1,576,192]{2,1,0:T(8,128)(2,1)}, bf16[1,576,192]{2,1,0:T(8,128)(2,1)S(1)}, u32[]{:S(2)}) copy-start(bf16[1,576,192]{2,1,0:T(8,128)(2,1)S(1)} %all-gather.10) | copy-start | bytes 663556
  231.9 7.8 copy-start.34
  234.1 6.8 copy-start.76
  237.4 11.3 copy-start.55
  237.4 13.6 copy-start.58
  239.7 205.0 %copy-start.7 = (f32[128,576]{0,1:T(8,128)}, f32[128,576]{0,1:T(8,128)S(1)}, u32[]{:S(2)}) copy-start(f32[128,576]{0,1:T(8,128)S(1)} %get-tuple-element.361) | copy-start | bytes 884740
  239.9 14.3 copy-start.9
  240.9 146.2 %all-gather.35.cloned.1.call-start = ((), (), s32[]{:S(2)}) async-start(), calls=%async_computation.19 | async-start | bytes 3194880 | tf_op jit(solution)/shard_map/all_gather | solution.py:116
  245.0 201.1 %all-gather.45.cloned.1.call-start = ((), (), s32[]{:S(2)}) async-start(), calls=%async_computation.40 | async-start | bytes 2654208 | tf_op jit(solution)/shard_map/all_gather | solution.py:356
  245.7 202.4 %all-gather.43.cloned.1.call-start = ((), (), s32[]{:S(2)}) async-start(), calls=%async_computation.39 | async-start | bytes 2654208 | tf_op jit(solution)/shard_map/all_gather | solution.py:355
  246.3 533.0 %reduce-scatter.17.cloned.1.call-start = ((), (), s32[]{:S(2)}) async-start(), calls=%async_computation.20 | async-start | bytes 12779520 | tf_op jit(solution)/shard_map/reduce_scatter | solution.py:268
  248.7 138.4 %copy-start.19 = (bf16[1,576,576]{2,1,0:T(8,128)(2,1)}, bf16[1,576,576]{2,1,0:T(8,128)(2,1)S(1)}, u32[]{:S(2)}) copy-start(bf16[1,576,576]{2,1,0:T(8,128)(2,1)S(1)} %all-gather.11) | copy-start | bytes 1990660
  251.0 193.7 %copy-start.21 = (bf16[1,576,576]{2,1,0:T(8,128)(2,1)}, bf16[1,576,576]{2,1,0:T(8,128)(2,1)S(1)}, u32[]{:S(2)}) copy-start(bf16[1,576,576]{2,1,0:T(8,128)(2,1)S(1)} %all-gather.13) | copy-start | bytes 1990660
  475.1 17.5 %copy-start.67 = (pred[128,8192]{0,1:T(8,128)(4,1)}, pred[128,8192]{0,1:T(8,128)(4,1)S(1)}, u32[]{:S(2)}) copy-start(pred[128,8192]{0,1:T(8,128)(4,1)S(1)} %fusion.37) | copy-start | bytes 3145732 | tf_op jit(solution)/shard_map/cond
  475.1 17.5 %copy-start.66 = (f32[128,3,3,64]{0,3,2,1:T(8,128)S(1)}, f32[128,3,3,64]{0,3,2,1:T(8,128)}, u32[]{:S(2)}) copy-start(f32[128,3,3,64]{0,3,2,1:T(8,128)} %get-tuple-element.187) | copy-start | bytes 884740 | tf_op jit(solution)/shard_map/cond
  550.6 349.9 %reduce-scatter.23.cloned.1.call-start = ((), (), s32[]{:S(2)}) async-start(), calls=%async_computation.23 | async-start | bytes 1105920 | tf_op jit(solution)/shard_map/reduce_scatter | solution.py:386
  553.1 351.2 %reduce-scatter.35.cloned.1.call-start = ((), (), s32[]{:S(2)}) async-start(), calls=%async_computation.29 | async-start | bytes 1105920 | tf_op jit(solution)/shard_map/reduce_scatter | solution.py:395
  554.5 351.8 %reduce-scatter.47.cloned.1.call-start = ((), (), s32[]{:S(2)}) async-start(), calls=%async_computation.35 | async-start | bytes 2654208 | tf_op jit(solution)/shard_map/reduce_scatter | solution.py:407
  556.4 352.4 %reduce-scatter.39.cloned.1.call-start = ((), (), s32[]{:S(2)}) async-start(), calls=%async_computation.31 | async-start | bytes 2654208 | tf_op jit(solution)/shard_map/reduce_scatter | solution.py:401
  558.3 222.0 %copy-start.31 = (bf16[1,576,192]{2,1,0:T(8,128)(2,1)S(1)}, bf16[1,576,192]{2,1,0:T(8,128)(2,1)}, u32[]{:S(2)}) copy-start(bf16[1,576,192]{2,1,0:T(8,128)(2,1)} %copy-done.30) | copy-start | bytes 663556
  558.3 222.2 %copy-start.8 = (f32[128,576]{0,1:T(8,128)S(1)}, f32[128,576]{0,1:T(8,128)}, u32[]{:S(2)}) copy-start(f32[128,576]{0,1:T(8,128)} %copy-done.7) | copy-start | bytes 884740
  558.3 222.2 %copy-start.33 = (bf16[1,576,192]{2,1,0:T(8,128)(2,1)S(1)}, bf16[1,576,192]{2,1,0:T(8,128)(2,1)}, u32[]{:S(2)}) copy-start(bf16[1,576,192]{2,1,0:T(8,128)(2,1)} %copy-done.32) | copy-start | bytes 663556
  558.3 353.0 %reduce-scatter.43.cloned.1.call-start = ((), (), s32[]{:S(2)}) async-start(), calls=%async_computation.33 | async-start | bytes 2654208 | tf_op jit(solution)/shard_map/reduce_scatter | solution.py:404
  560.2 353.7 %reduce-scatter.27.cloned.1.call-start = ((), (), s32[]{:S(2)}) async-start(), calls=%async_computation.25 | async-start | bytes 442368 | tf_op jit(solution)/shard_map/reduce_scatter | solution.py:389
  784.9 6.6 copy-start
  784.9 6.6 copy-start.87
  787.9 127.7 %reduce-scatter.31.cloned.1.call-start = ((), (), s32[]{:S(2)}) async-start(), calls=%async_computation.27 | async-start | bytes 442368 | tf_op jit(solution)/shard_map/reduce_scatter | solution.py:392
  791.5 97.4 %copy-start.12 = (bf16[128,576]{0,1:T(8,128)(2,1)S(1)}, bf16[128,576]{0,1:T(8,128)(2,1)}, u32[]{:S(2)}) copy-start(bf16[128,576]{0,1:T(8,128)(2,1)} %copy-done.9) | copy-start | bytes 442372
  791.5 100.5 %copy-start.3 = (bf16[128,576]{0,1:T(8,128)(2,1)S(1)}, bf16[128,576]{0,1:T(8,128)(2,1)}, u32[]{:S(2)}) copy-start(bf16[128,576]{0,1:T(8,128)(2,1)} %param.20) | copy-start | bytes 442372
  791.5 100.5 %copy-start.83 = (f32[576]{0:T(1024)S(1)}, f32[576]{0:T(1024)}, u32[]{:S(2)}) copy-start(f32[576]{0:T(1024)} %copy-done.82) | copy-start | bytes 6916
  791.5 100.5 %copy-start.85 = (f32[128]{0:T(128)S(1)}, f32[128]{0:T(128)}, u32[]{:S(2)}) copy-start(f32[128]{0:T(128)} %copy-done.84) | copy-start | bytes 1540
  812.7 17.8 %copy-start.68 = (pred[128,8192]{0,1:T(8,128)(4,1)}, pred[128,8192]{0,1:T(8,128)(4,1)S(1)}, u32[]{:S(2)}) copy-start(pred[128,8192]{0,1:T(8,128)(4,1)S(1)} %fusion.49) | copy-start | bytes 3145732 | tf_op jit(solution)/shard_map/cond
  812.7 17.8 %copy-start.65 = (f32[128,3,3,64]{0,3,2,1:T(8,128)S(1)}, f32[128,3,3,64]{0,3,2,1:T(8,128)}, u32[]{:S(2)}) copy-start(f32[128,3,3,64]{0,3,2,1:T(8,128)} %get-tuple-element.197) | copy-start | bytes 884740 | tf_op jit(solution)/shard_map/cond
  888.9 6.8 copy-start.35
  888.9 6.8 copy-start.52
  890.9 26.4 %reduce-scatter.21.cloned.1.call-start = ((), (), s32[]{:S(2)}) async-start(), calls=%async_computation.22 | async-start | bytes 1105920 | tf_op jit(solution)/shard_map/reduce_scatter | solution.py:386
  893.3 37.3 %reduce-scatter.33.cloned.1.call-start = ((), (), s32[]{:S(2)}) async-start(), calls=%async_computation.28 | async-start | bytes 1105920 | tf_op jit(solution)/shard_map/reduce_scatter | solution.py:395
  895.6 51.4 %reduce-scatter.37.cloned.1.call-start = ((), (), s32[]{:S(2)}) async-start(), calls=%async_computation.30 | async-start | bytes 2654208 | tf_op jit(solution)/shard_map/reduce_scatter | solution.py:401
  897.5 283.5 %reduce-scatter.19.cloned.1.call-start = ((), (), s32[]{:S(2)}) async-start(), calls=%async_computation.21 | async-start | bytes 12779520 | tf_op jit(solution)/shard_map/reduce_scatter | solution.py:268
  898.3 296.7 %reduce-scatter.41.cloned.1.call-start = ((), (), s32[]{:S(2)}) async-start(), calls=%async_computation.32 | async-start | bytes 2654208 | tf_op jit(solution)/shard_map/reduce_scatter | solution.py:404
  900.4 310.3 %reduce-scatter.45.cloned.1.call-start = ((), (), s32[]{:S(2)}) async-start(), calls=%async_computation.34 | async-start | bytes 2654208 | tf_op jit(solution)/shard_map/reduce_scatter | solution.py:407
  904.3 321.2 %reduce-scatter.25.cloned.1.call-start = ((), (), s32[]{:S(2)}) async-start(), calls=%async_computation.24 | async-start | bytes 442368 | tf_op jit(solution)/shard_map/reduce_scatter | solution.py:389
  1183.0 56.4 %reduce-scatter.29.cloned.1.call-start = ((), (), s32[]{:S(2)}) async-start(), calls=%async_computation.26 | async-start | bytes 442368 | tf_op jit(solution)/shard_map/reduce_scatter | solution.py:392
  1199.6 273.9 %all-reduce.14.cloned.1.call-start = ((), (), s32[]{:S(2)}) async-start(), calls=%async_computation.42 | async-start | bytes 29491200 | tf_op jit(solution)/shard_map/psum | solution.py:411
  1241.1 165.8 %copy-start.24 = (f32[128,576]{0,1:T(8,128)S(1)}, f32[128,576]{0,1:T(8,128)}, u32[]{:S(2)}) copy-start(f32[128,576]{0,1:T(8,128)} %copy-done.23) | copy-start | bytes 884740
  1241.1 165.8 %copy-start.90 = (f32[128]{0:T(128)S(1)}, f32[128]{0:T(128)}, u32[]{:S(2)}) copy-start(f32[128]{0:T(128)} %get-tuple-element.346) | copy-start | bytes 1540
  1473.4 6.1 copy-start.78
  1473.4 6.1 copy-start.79
  1473.5 6.0 copy-start.80
  (55 other events, 176.8 us)
Sparse Core Ops, SparseCore 0:
  24.5 73.4 all-gather.28
  101.3 71.4 all-gather.30
  175.0 13.3 all-gather.36
  190.5 14.1 all-gather.38
  206.1 14.1 all-gather.40
  222.4 14.1 all-gather.46
  241.0 71.3 all-gather.32
  315.6 71.4 all-gather.34
  389.4 13.3 all-gather.44
  404.8 14.1 all-gather.42
  550.7 228.5 reduce-scatter.16
  781.6 10.5 reduce-scatter.22
  794.5 12.2 reduce-scatter.34
  809.0 13.2 reduce-scatter.46
  825.3 13.3 reduce-scatter.38
  841.4 13.2 reduce-scatter.42
  857.1 11.7 reduce-scatter.26
  891.0 9.6 reduce-scatter.30
  903.8 12.2 reduce-scatter.20
  918.4 12.1 reduce-scatter.32
  933.7 13.2 reduce-scatter.36
  951.6 229.3 reduce-scatter.18
  1183.4 11.6 reduce-scatter.40
  1197.4 13.2 reduce-scatter.44
  1213.6 11.7 reduce-scatter.24
  1227.7 11.7 reduce-scatter.28
  1246.8 226.5 all-reduce.13
where the time goes:
time: 1500 us; the launch traced here: 1490 us
  waiting for transfers between devices  848 us (57%)
  matrix products  287 us (19%)
  blocking collectives  181 us (12%)
  other arithmetic  133 us (9%)
  local copies, waits for them, and re-layouts  23 us (2%)
  between operations  18.6 us (1%)
    reduce_scatter x2, waiting for transfers between devices, backward_layer(): lax.psum_scatter(buffer, 'rep', scatter_dimension=0, tiled=True)  450 us
    psum x1, blocking collectives, per_device(): lax.psum((owned[0], owned[1], owned[2], owned[3], owned[4], owned[5], own...  156 us
    all_gather x2, waiting for transfers between devices, forward_layer(): value_slice = lax.all_gather(values_now, 'rep', axis=0, tiled=True)  149 us
    all_gather x2, waiting for transfers between devices, forward_layer(): key_slice = lax.all_gather(keys_now, 'rep', axis=0, tiled=True)  106 us
    dot_general x4, matrix products, piece_scores(): jnp.einsum('tkgd,rkd->tkgr', query_rows, key_slice.reshape(token_count, K...  66 us
    psum x1, waiting for transfers between devices, per_device(): lax.psum((owned[0], owned[1], owned[2], owned[3], owned[4], owned[5], own...  65.7 us
    dot_general x2, matrix products, backward_update(): jnp.einsum('tkgd,rkd->tkgr', grad_attended, value_slice.reshape(token_cou...  52.2 us
    another operation x20, other arithmetic, per_device(): jnp.stack([collected[layer_no][member] for layer_no in range(DECODER_LAYE...  41.5 us
  transfers between devices with their start and end apart: 27, of which 13 were waited for; matrix products, arithmetic and copies ran while one was open for 21% of the time, Pallas kernels for 0%

commit v1 on v0

v1 whole, which is shorter than its diff:
```python
import functools
import math

import jax
import jax.numpy as jnp
from jax import lax
from jax.experimental import pallas as pl
from jax.experimental.pallas import tpu as pltpu
from jax.sharding import PartitionSpec as P

QUERY_HEADS = 9
KEY_VALUE_HEADS = 3
HEAD_SIZE = 64
DECODER_LAYERS = 2
MODEL_WIDTH = 576
HALF = 64
EPSILON = 1e-05
LOWEST = -1e30
FLOOR = -1e20

MESH = pl.DeviceIdType.MESH
ANY = pl.BlockSpec(memory_space=pl.ANY)
VMEM = pl.BlockSpec(memory_space=pltpu.VMEM)


def coords():
    rep = lax.axis_index("rep")
    return lax.axis_index("shard"), rep // 16, (rep // 4) % 4, rep % 4


def device(core, x, z, y):
    return (core, x * 16 + z * 4 + y)


def line_peer(axis, step):
    core, x, z, y = coords()
    if axis == "x":
        return device(core, (x + step) % 4, z, y)
    if axis == "z":
        return device(core, x, (z + step) % 4, y)
    return device(core, x, z, (y + step) % 4)


def core_peer():
    core, x, z, y = coords()
    return device(1 - core, x, z, y)


def mirror_peer():
    core, x, z, y = coords()
    return device(core, 3 - x, 3 - z, 3 - y)


def greet(peers):
    barrier = pltpu.get_barrier_semaphore()
    for peer in peers:
        pl.semaphore_signal(barrier, inc=1, device_id=peer, device_id_type=MESH)
    pl.semaphore_wait(barrier, len(peers))


def line_peers(axes):
    return [line_peer(axis, step) for axis in axes for step in (1, 2, 3)]


class Copies:
    def __init__(self, send, recv, local):
        self.send, self.recv, self.local = send, recv, local
        self.remotes, self.locals = 0, 0

    def remote(self, src, dst, peer):
        copy = pltpu.make_async_remote_copy(
            src_ref=src,
            dst_ref=dst,
            send_sem=self.send.at[self.remotes],
            recv_sem=self.recv.at[self.remotes],
            device_id=peer,
            device_id_type=MESH,
        )
        self.remotes += 1
        copy.start()
        return copy

    def here(self, src, dst):
        copy = pltpu.make_async_copy(src, dst, self.local.at[self.locals])
        self.locals += 1
        copy.start()
        return copy


def comm_call(kernel, name, cid, args, outs, in_specs, out_specs, remotes, locals_, scratch=()):
    return pl.pallas_call(
        kernel,
        out_shape=outs,
        in_specs=in_specs,
        out_specs=out_specs,
        scratch_shapes=[
            pltpu.SemaphoreType.DMA((remotes,)),
            pltpu.SemaphoreType.DMA((remotes,)),
            pltpu.SemaphoreType.DMA((max(locals_, 1),)),
            *scratch,
        ],
        compiler_params=pltpu.CompilerParams(
            collective_id=cid, has_side_effects=True, vmem_limit_bytes=56 << 20
        ),
        name=name,
    )(*args)


def shape_of(shape, dtype):
    return jax.ShapeDtypeStruct(shape, dtype)


def start_kernel(weights, *refs):
    tokens, cotangent, gains = refs[:3]
    mine = refs[3 : 3 + weights]
    tokens_out, cotangent_out, gains_out = refs[3 + weights : 6 + weights]
    both = refs[6 + weights : 6 + 2 * weights]
    copies = Copies(*refs[6 + 2 * weights :])
    core = lax.axis_index("shard")
    other, mirror = core_peer(), mirror_peer()
    greet([other, mirror])
    low, high = pl.ds(0, HALF), pl.ds(HALF, HALF)
    started = [copies.remote(tokens.at[high], tokens_out.at[high], mirror)]
    started.append(copies.remote(gains, gains_out.at[core], other))
    for own, all_ in zip(mine, both):
        started.append(copies.remote(own.at[0], all_.at[core], other))
    started.append(copies.remote(cotangent.at[high], cotangent_out.at[high], mirror))
    started.append(copies.here(tokens.at[low], tokens_out.at[low]))
    started.append(copies.here(cotangent.at[low], cotangent_out.at[low]))
    started.append(copies.here(gains, gains_out.at[core]))
    for own, all_ in zip(mine, both):
        started.append(copies.here(own.at[0], all_.at[core]))
    for copy in started:
        copy.wait()


def start(tokens, cotangent, gains, weights):
    outs = [
        shape_of(tokens.shape, tokens.dtype),
        shape_of(cotangent.shape, cotangent.dtype),
        shape_of((2,) + gains.shape, gains.dtype),
        *[shape_of((2,) + w.shape[1:], w.dtype) for w in weights],
    ]
    count = len(weights)
    return comm_call(
        functools.partial(start_kernel, count),
        "start_rows",
        0,
        (tokens, cotangent, gains, *weights),
        outs,
        [ANY] * (3 + count),
        [ANY] * (3 + count),
        3 + count,
        3 + count,
    )


def gather_kernel(layers, *refs):
    weights = len(layers)
    queries, even, odd = refs[:3]
    mine = refs[3 : 3 + weights]
    queries_all, even_all, odd_all = refs[3 + weights : 6 + weights]
    both = refs[6 + weights : 6 + 2 * weights]
    copies = Copies(*refs[6 + 2 * weights :])
    core, x, z, y = coords()
    other = core_peer()
    greet([other, *line_peers("xzy")])
    first_even = [copies.remote(even, even_all.at[z, y], line_peer("y", d)) for d in (1, 2, 3)]
    first_odd = [copies.remote(odd, odd_all.at[y, z], line_peer("z", d)) for d in (1, 2, 3)]
    first_even.append(copies.here(even, even_all.at[z, y]))
    first_odd.append(copies.here(odd, odd_all.at[y, z]))
    rest = [copies.remote(queries, queries_all.at[x], line_peer("x", d)) for d in (1, 2, 3)]
    rest.append(copies.here(queries, queries_all.at[x]))
    for layer, own, all_ in zip(layers, mine, both):
        rest.append(copies.remote(own.at[layer], all_.at[core], other))
        rest.append(copies.here(own.at[layer], all_.at[core]))
    for copy in first_even:
        copy.wait()
    for d in (1, 2, 3):
        rest.append(copies.remote(even_all.at[z], even_all.at[z], line_peer("z", d)))
    for copy in first_odd:
        copy.wait()
    for d in (1, 2, 3):
        rest.append(copies.remote(odd_all.at[y], odd_all.at[y], line_peer("y", d)))
    for copy in rest:
        copy.wait()


def gather(queries, even, odd, weights, layers, cid):
    kv = even.shape[1]
    outs = [
        shape_of((4,) + queries.shape, queries.dtype),
        shape_of((4, 4, HALF, kv), even.dtype),
        shape_of((4, 4, HALF, kv), odd.dtype),
        *[shape_of((2,) + w.shape[1:], w.dtype) for w in weights],
    ]
    count = len(weights)
    return comm_call(
        functools.partial(gather_kernel, tuple(layers)),
        f"gather_qkv_{cid}",
        cid,
        (queries, even, odd, *weights),
        outs,
        [ANY] * (3 + count),
        [ANY] * (3 + count),
        15 + count,
        3 + count,
    )


def unit_places(step):
    x = lax.axis_index("rep") // 16
    in_odd = step >= 4 - x
    section = jnp.where(in_odd, 1, 0)
    quarter = jnp.where(in_odd, step - 1, x + step)
    return section, quarter


def unit_bias(section, quarter, starts_ref):
    rep = lax.axis_index("rep")
    x, line = rep // 16, rep % 16
    row = lax.broadcasted_iota(jnp.int32, (1024, 128), 0)
    block, inside = row // HALF, row % HALF
    even_key = (16 * x + block) * 128 + inside
    odd_key = (127 - 2 * (16 * x + (block % 4) * 4 + block // 4)) * HALF + inside
    key = jnp.where(section == 1, odd_key, even_key)
    lane = lax.broadcasted_iota(jnp.int32, (1, 128), 1)
    even_query = (16 * quarter + line) * 128 + lane
    odd_query = (127 - 2 * (16 * (3 - quarter) + line)) * HALF + lane - HALF
    query = jnp.where(lane < HALF, even_query, odd_query)
    begin = jnp.where(
        lane < HALF, starts_ref[pl.ds(quarter, 1), :], starts_ref[pl.ds(3 - quarter, 1), :]
    )
    return jnp.where((key <= query) & (key >= begin), 0.0, LOWEST)


def head_rows(ref, quarter, group):
    parts = []
    for head in range(3 * group, 3 * group + 3):
        columns = slice(head * HEAD_SIZE, (head + 1) * HEAD_SIZE)
        parts.append(ref[quarter, 0:HALF, columns])
        parts.append(ref[3 - quarter, HALF : 2 * HALF, columns])
    return jnp.concatenate(parts, axis=0)


def contract(left, right, left_dim, right_dim):
    return lax.dot_general(
        left, right, (((left_dim,), (right_dim,)), ((), ())), preferred_element_type=jnp.float32
    )


def attend_kernel(q_ref, even_ref, odd_ref, starts_ref, o_ref, lse_ref, bias, best, total, accum):
    best[...] = jnp.full(best.shape, FLOOR, jnp.float32)
    total[...] = jnp.zeros(total.shape, jnp.float32)
    accum[...] = jnp.zeros(accum.shape, jnp.float32)

    def unit(section, quarter, kv_ref):
        bias[...] = unit_bias(section, quarter, starts_ref)
        for group in range(3):
            queries = head_rows(q_ref, quarter, group)
            keys = kv_ref[:, group * 128 : group * 128 + 64]
            values = kv_ref[:, group * 128 + 64 : group * 128 + 128]
            scores = contract(keys, queries, 1, 1)
            tile = bias[...]
            scores = scores + jnp.concatenate([tile, tile, tile], axis=1)
            old = best[quarter, group]
            new = jnp.maximum(old, jnp.max(scores, axis=0, keepdims=True))
            expon = jnp.exp(scores - new)
            decay = jnp.exp(old - new)
            best[quarter, group] = new
            total[quarter, group] = total[quarter, group] * decay + jnp.sum(
                expon, axis=0, keepdims=True
            )
            accum[quarter, group] = accum[quarter, group] * decay + contract(
                values, expon.astype(jnp.bfloat16), 0, 0
            )

    def step_body(step, carry):
        section, quarter = unit_places(step)

        @pl.when(section == 0)
        def _():
            unit(section, quarter, even_ref)

        @pl.when(section == 1)
        def _():
            unit(section, quarter, odd_ref)

        return carry

    lax.fori_loop(0, 5, step_body, 0)
    lane = lax.broadcasted_iota(jnp.int32, (1, 128), 1)
    results, logs = {}, {}
    for quarter in range(4):
        for group in range(3):
            summed = total[quarter, group]
            safe = jnp.where(summed > 0.0, summed, 1.0)
            results[quarter, group] = accum[quarter, group] / safe
            logs[quarter, group] = best[quarter, group] + jnp.log(safe)
    for chunk in range(4):
        rows = []
        for head in range(QUERY_HEADS):
            group, part = head // 3, slice((head % 3) * 128, (head % 3) * 128 + 128)
            o_ref[chunk, head * 64 : head * 64 + 64, :] = jnp.where(
                lane < HALF, results[chunk, group][:, part], results[3 - chunk, group][:, part]
            ).astype(jnp.bfloat16)
            rows.append(
                jnp.where(lane < HALF, logs[chunk, group][:, part], logs[3 - chunk, group][:, part])
            )
        rows.append(jnp.zeros((7, 128), jnp.float32))
        lse_ref[chunk] = jnp.concatenate(rows, axis=0)


def attend(queries, even, odd, starts):
    return pl.pallas_call(
        attend_kernel,
        out_shape=[
            shape_of((4, MODEL_WIDTH, 128), jnp.bfloat16),
            shape_of((4, 16, 128), jnp.float32),
        ],
        in_specs=[VMEM] * 4,
        out_specs=[VMEM] * 2,
        scratch_shapes=[
            pltpu.VMEM((1024, 128), jnp.float32),
            pltpu.VMEM((4, 3, 1, 384), jnp.float32),
            pltpu.VMEM((4, 3, 1, 384), jnp.float32),
            pltpu.VMEM((4, 3, 64, 384), jnp.float32),
        ],
        compiler_params=pltpu.CompilerParams(vmem_limit_bytes=56 << 20),
        name="attend",
    )(queries, even.reshape(1024, 384), odd.reshape(1024, 384), starts)


def merge_kernel(o_ref, lse_ref, o_all, lse_all, send, recv, local):
    copies = Copies(send, recv, local)
    _, x, _, _ = coords()
    greet(line_peers("x"))
    started = []
    for d in (1, 2, 3):
        peer = (x + d) % 4
        started.append(copies.remote(o_ref.at[peer], o_all.at[x], line_peer("x", d)))
        started.append(copies.remote(lse_ref.at[peer], lse_all.at[x], line_peer("x", d)))
    started.append(copies.here(o_ref.at[x], o_all.at[x]))
    started.append(copies.here(lse_ref.at[x], lse_all.at[x]))
    for copy in started:
        copy.wait()


def exchange_partials(partial, logs, cid):
    return comm_call(
        merge_kernel,
        f"swap_partials_{cid}",
        cid,
        (partial, logs),
        [shape_of(partial.shape, partial.dtype), shape_of(logs.shape, logs.dtype)],
        [ANY] * 2,
        [ANY] * 2,
        6,
        2,
    )


def back_gather_kernel(halves, wholes, *refs):
    count = halves + wholes
    grads, stats = refs[:2]
    mine = refs[2 : 2 + count]
    grads_all, stats_all = refs[2 + count : 4 + count]
    both = refs[4 + count : 4 + 2 * count]
    copies = Copies(*refs[4 + 2 * count :])
    core, x, _, _ = coords()
    other = core_peer()
    greet([other, *line_peers("x")])
    started = []
    for d in (1, 2, 3):
        started.append(copies.remote(grads, grads_all.at[x], line_peer("x", d)))
        started.append(copies.remote(stats, stats_all.at[x], line_peer("x", d)))
    started.append(copies.here(grads, grads_all.at[x]))
    started.append(copies.here(stats, stats_all.at[x]))
    for at, (own, all_) in enumerate(zip(mine, both)):
        if at < halves:
            started.append(copies.remote(own.at[1 - core], all_.at[core], other))
            started.append(copies.here(own.at[core], all_.at[core]))
        else:
            started.append(copies.remote(own, all_.at[core], other))
            started.append(copies.here(own, all_.at[core]))
    for copy in started:
        copy.wait()


def back_gather(grads, stats, halves, wholes, cid):
    count = len(halves) + len(wholes)
    return comm_call(
        functools.partial(back_gather_kernel, len(halves), len(wholes)),
        f"gather_grads_{cid}",
        cid,
        (grads, stats, *halves, *wholes),
        [
            shape_of((4,) + grads.shape, grads.dtype),
            shape_of((4,) + stats.shape, stats.dtype),
            *[shape_of(item.shape, item.dtype) for item in halves],
            *[shape_of((2,) + item.shape, item.dtype) for item in wholes],
        ],
        [ANY] * (2 + count),
        [ANY] * (2 + count),
        6 + count,
        2 + count,
    )


def attend_back_kernel(
    q_ref, even_ref, odd_ref, do_ref, stats_ref, starts_ref, dq_ref, dkv_ref, bias, dq, dkv
):
    dq[...] = jnp.zeros(dq.shape, jnp.float32)
    dkv[...] = jnp.zeros(dkv.shape, jnp.float32)

    def unit(section, quarter, kv_ref):
        bias[...] = unit_bias(section, quarter, starts_ref)
        lane = lax.broadcasted_iota(jnp.int32, (1, 128), 1)
        stats = jnp.where(lane < HALF, stats_ref[quarter], stats_ref[3 - quarter])
        for group in range(3):
            queries = head_rows(q_ref, quarter, group)
            grads = head_rows(do_ref, quarter, group)
            keys = kv_ref[:, group * 128 : group * 128 + 64]
            values = kv_ref[:, group * 128 + 64 : group * 128 + 128]
            heads = range(3 * group, 3 * group + 3)
            logs = jnp.concatenate([stats[0, h : h + 1, :] for h in heads], axis=1)
            delta = jnp.concatenate([stats[1, h : h + 1, :] for h in heads], axis=1)
            scores = contract(keys, queries, 1, 1)
            tile = bias[...]
            scores = scores + jnp.concatenate([tile, tile, tile], axis=1)
            weights = jnp.exp(scores - logs)
            grad_weights = contract(values, grads, 1, 1)
            grad_scores = (weights * (grad_weights - delta)).astype(jnp.bfloat16)
            grad_values = contract(weights.astype(jnp.bfloat16), grads, 1, 0)
            grad_keys = contract(grad_scores, queries, 1, 0)
            dkv[section, group] += jnp.concatenate([grad_keys, grad_values], axis=1)
            dq[quarter, group] += contract(keys, grad_scores, 0, 0)

    def step_body(step, carry):
        section, quarter = unit_places(step)

        @pl.when(section == 0)
        def _():
            unit(section, quarter, even_ref)

        @pl.when(section == 1)
        def _():
            unit(section, quarter, odd_ref)

        return carry

    lax.fori_loop(0, 5, step_body, 0)
    lane = lax.broadcasted_iota(jnp.int32, (1, 128), 1)
    for chunk in range(4):
        for head in range(QUERY_HEADS):
            group, part = head // 3, slice((head % 3) * 128, (head % 3) * 128 + 128)
            picked = jnp.where(
                lane < HALF, dq[chunk, group][:, part], dq[3 - chunk, group][:, part]
            )
            dq_ref[chunk, head * 64 : head * 64 + 64, :] = (picked * 0.125).astype(jnp.bfloat16)
    for section in range(2):
        for group in range(3):
            dkv_ref[section, :, group * 128 : group * 128 + 128] = dkv[section, group].astype(
                jnp.bfloat16
            )


def attend_back(queries, even, odd, grads, stats, starts):
    return pl.pallas_call(
        attend_back_kernel,
        out_shape=[
            shape_of((4, MODEL_WIDTH, 128), jnp.bfloat16),
            shape_of((2, 1024, 384), jnp.bfloat16),
        ],
        in_specs=[VMEM] * 6,
        out_specs=[VMEM] * 2,
        scratch_shapes=[
            pltpu.VMEM((1024, 128), jnp.float32),
            pltpu.VMEM((4, 3, 64, 384), jnp.float32),
            pltpu.VMEM((2, 3, 1024, 128), jnp.float32),
        ],
        compiler_params=pltpu.CompilerParams(vmem_limit_bytes=56 << 20),
        name="attend_back",
    )(queries, even.reshape(1024, 384), odd.reshape(1024, 384), grads, stats, starts)


def back_sum_kernel(dq_ref, dkv_ref, dq_out, dkv_out, send, recv, local, dq_in, first, middle, second):
    copies = Copies(send, recv, local)
    _, x, z, y = coords()
    greet(line_peers("xzy"))
    stage_one = [[], []]
    dq_copies = []
    for d in (1, 2, 3):
        stage_one[0].append(
            copies.remote(dkv_ref.at[0, (z + d) % 4], first.at[0, d - 1], line_peer("z", d))
        )
        stage_one[1].append(
            copies.remote(dkv_ref.at[1, (y + d) % 4], first.at[1, d - 1], line_peer("y", d))
        )
    for d in (1, 2, 3):
        dq_copies.append(copies.remote(dq_ref.at[(x + d) % 4], dq_in.at[d - 1], line_peer("x", d)))
    stage_two = [[], []]
    for half, mine, axis, there in ((0, z, "y", y), (1, y, "z", z)):
        for copy in stage_one[half]:
            copy.wait()
        total = dkv_ref[half, mine].astype(jnp.float32)
        for d in range(3):
            total = total + first[half, d].astype(jnp.float32)
        middle[half] = total.astype(jnp.bfloat16)
        for d in (1, 2, 3):
            stage_two[half].append(
                copies.remote(
                    middle.at[half, (there + d) % 4], second.at[half, d - 1], line_peer(axis, d)
                )
            )
    for copy in dq_copies:
        copy.wait()
    total = dq_ref[x].astype(jnp.float32)
    for d in range(3):
        total = total + dq_in[d].astype(jnp.float32)
    dq_out[...] = total
    for half, there in ((0, y), (1, z)):
        for copy in stage_two[half]:
            copy.wait()
        total = middle[half, there].astype(jnp.float32)
        for d in range(3):
            total = total + second[half, d].astype(jnp.float32)
        dkv_out[half * HALF : (half + 1) * HALF, :] = total


def back_sum(dq, dkv, cid):
    return comm_call(
        back_sum_kernel,
        f"sum_dqkv_{cid}",
        cid,
        (dq, dkv.reshape(2, 4, 4, HALF, 384)),
        [shape_of((MODEL_WIDTH, 128), jnp.float32), shape_of((128, 384), jnp.float32)],
        [VMEM] * 2,
        [VMEM] * 2,
        15,
        1,
        [
            pltpu.VMEM((3, MODEL_WIDTH, 128), jnp.bfloat16),
            pltpu.VMEM((2, 3, 4, HALF, 384), jnp.bfloat16),
            pltpu.VMEM((2, 4, HALF, 384), jnp.bfloat16),
            pltpu.VMEM((2, 3, HALF, 384), jnp.bfloat16),
        ],
    )


def pair_kernel(qkv, gains, qkv_all, gains_all, send, recv, local):
    copies = Copies(send, recv, local)
    core = lax.axis_index("shard")
    other = core_peer()
    greet([other])
    started = [
        copies.remote(qkv, qkv_all.at[core], other),
        copies.remote(gains.at[1 - core], gains_all.at[core], other),
        copies.here(qkv, qkv_all.at[core]),
        copies.here(gains.at[core], gains_all.at[core]),
    ]
    for copy in started:
        copy.wait()


def pair_exchange(qkv, gains, cid):
    return comm_call(
        pair_kernel,
        f"swap_cores_{cid}",
        cid,
        (qkv, gains),
        [shape_of((2,) + qkv.shape, qkv.dtype), shape_of(gains.shape, gains.dtype)],
        [ANY] * 2,
        [ANY] * 2,
        2,
        2,
    )


GRAD_ROWS = 1216
PIECE = GRAD_ROWS // 4


def weight_grad_kernel(
    normed, attended, normed_two, inner, branch, gate, up, middle, qkv, gains, out
):
    def rows(ref):
        return ref[...].reshape(ref.shape[0] * ref.shape[1], ref.shape[2])

    grad_qkv = contract(rows(normed), rows(qkv), 0, 0)
    grad_out = contract(rows(attended), rows(middle), 0, 0)
    out[0:288, :] = jnp.concatenate([grad_qkv, grad_out], axis=1).astype(jnp.bfloat16)
    two = rows(normed_two)
    out[288:576, :] = contract(two, rows(gate), 0, 0).astype(jnp.bfloat16)
    out[576:864, :] = contract(two, rows(up), 0, 0).astype(jnp.bfloat16)
    down = contract(rows(branch), rows(inner), 0, 0).astype(jnp.bfloat16)
    out[864:1152, 0:768] = down[0:288]
    out[864:1152, 768:1536] = down[288:576]
    out[1152:GRAD_ROWS, :] = jnp.zeros((GRAD_ROWS - 1152, 1536), jnp.bfloat16)
    out[1152:1168, 0:384] = (gains[0] + gains[1]).astype(jnp.bfloat16)


def weight_grads(*args):
    return pl.pallas_call(
        weight_grad_kernel,
        out_shape=shape_of((GRAD_ROWS, 1536), jnp.bfloat16),
        in_specs=[VMEM] * len(args),
        out_specs=VMEM,
        compiler_params=pltpu.CompilerParams(vmem_limit_bytes=56 << 20),
        name="weight_grads",
    )(*args)


def reduce_kernel(g_ref, out_ref, send, recv, local, one, sum_one, two, three):
    copies = Copies(send, recv, local)
    _, x, z, y = coords()
    place = {"x": x, "z": z, "y": y}
    orders = ("xzy", "zyx", "yxz")
    greet(line_peers("xzy"))

    def columns(part, at):
        return pl.ds(pl.multiple_of(part * 512 + at * 128, 128), 128)

    def rows(at):
        return pl.ds(pl.multiple_of(at * PIECE, 16), PIECE)

    stages = [[], [], []]
    for part, order in enumerate(orders):
        axis = order[0]
        for d in (1, 2, 3):
            stages[part].append(
                copies.remote(
                    g_ref.at[:, columns(part, (place[axis] + d) % 4)],
                    one.at[part, d - 1],
                    line_peer(axis, d),
                )
            )
    for part, order in enumerate(orders):
        for copy in stages[part]:
            copy.wait()
        total = g_ref[:, columns(part, place[order[0]])].astype(jnp.float32)
        for d in range(3):
            total = total + one[part, d].astype(jnp.float32)
        sum_one[part] = total.astype(jnp.bfloat16)
        axis = order[1]
        stages[part] = [
            copies.remote(
                sum_one.at[part, rows((place[axis] + d) % 4)],
                two.at[part, d - 1],
                line_peer(axis, d),
            )
            for d in (1, 2, 3)
        ]
    for part, order in enumerate(orders):
        for copy in stages[part]:
            copy.wait()
        total = sum_one[part, rows(place[order[1]])].astype(jnp.float32)
        for d in range(3):
            total = total + two[part, d].astype(jnp.float32)
        axis = order[2]
        here = place[axis]
        three[part, here] = total.astype(jnp.bfloat16)
        stages[part] = [
            copies.remote(three.at[part, here], three.at[part, here], line_peer(axis, d))
            for d in (1, 2, 3)
        ]
    for part, order in enumerate(orders):
        for copy in stages[part]:
            copy.wait()
        total = three[part, 0].astype(jnp.float32)
        for at in (1, 2, 3):
            total = total + three[part, at].astype(jnp.float32)
        window = (rows(place[order[1]]), columns(part, place[order[0]]))
        out_ref[window] = total.astype(jnp.bfloat16)
        stages[part] = [
            copies.remote(out_ref.at[window], out_ref.at[window], line_peer(order[1], d))
            for d in (1, 2, 3)
        ]
    for part, order in enumerate(orders):
        for copy in stages[part]:
            copy.wait()
        window = (slice(None), columns(part, place[order[0]]))
        stages[part] = [
            copies.remote(out_ref.at[window], out_ref.at[window], line_peer(order[0], d))
            for d in (1, 2, 3)
        ]
    for part in range(3):
        for copy in stages[part]:
            copy.wait()


def reduce_grads(grads, cid):
    return comm_call(
        reduce_kernel,
        f"sum_weight_grads_{cid}",
        cid,
        (grads,),
        shape_of(grads.shape, grads.dtype),
        [VMEM],
        VMEM,
        45,
        1,
        [
            pltpu.VMEM((3, 3, GRAD_ROWS, 128), jnp.bfloat16),
            pltpu.VMEM((3, GRAD_ROWS, 128), jnp.bfloat16),
            pltpu.VMEM((3, 3, PIECE, 128), jnp.bfloat16),
            pltpu.VMEM((3, 4, PIECE, 128), jnp.bfloat16),
        ],
    )


def finish_kernel(acts, grads, acts_out, grads_out, send, recv, local):
    copies = Copies(send, recv, local)
    mirror = mirror_peer()
    greet([mirror])
    low, high = pl.ds(0, HALF), pl.ds(HALF, HALF)
    started = [
        copies.remote(grads.at[high], grads_out.at[high], mirror),
        copies.remote(acts.at[high], acts_out.at[high], mirror),
        copies.here(grads.at[low], grads_out.at[low]),
        copies.here(acts.at[low], acts_out.at[low]),
    ]
    for copy in started:
        copy.wait()


def finish(acts, grads, cid):
    return comm_call(
        finish_kernel,
        "return_rows",
        cid,
        (acts, grads),
        [shape_of(acts.shape, acts.dtype), shape_of(grads.shape, grads.dtype)],
        [ANY] * 2,
        [ANY] * 2,
        2,
        2,
    )


def sequence_starts(lengths, rows):
    ends = jnp.cumsum(lengths)
    begins = ends - lengths
    segment = jnp.sum((rows[..., None] >= ends).astype(jnp.int32), axis=-1)
    labels = jnp.arange(lengths.shape[0], dtype=jnp.int32)
    return jnp.sum(jnp.where(segment[..., None] == labels, begins, 0), axis=-1)


def rope_tables(position):
    half = HEAD_SIZE // 2
    freqs = jnp.exp(jnp.arange(half, dtype=jnp.float32) * (-2.0 * math.log(10000.0) / HEAD_SIZE))
    angles = position.astype(jnp.float32)[:, None] * freqs[None, :]
    return jnp.cos(angles), jnp.sin(angles)


def rope(rows, tables, sign):
    cosine, sine = tables
    half = HEAD_SIZE // 2
    shaped = rows.reshape(rows.shape[0], -1, HEAD_SIZE)
    one, two = shaped[..., :half], shaped[..., half:]
    cosine, sine = cosine[:, None, :], sign * sine[:, None, :]
    return jnp.concatenate(
        [one * cosine - two * sine, two * cosine + one * sine], axis=-1
    ).reshape(rows.shape)


def dot(left, right):
    return jnp.dot(left, right, preferred_element_type=jnp.float32)


def dot_t(left, right):
    return jnp.einsum("ta,ba->tb", left, right, preferred_element_type=jnp.float32)


def inverse_rms(rows):
    return lax.rsqrt(jnp.mean(rows * rows, axis=-1, keepdims=True) + EPSILON)


def norm_back(grad, rows, inverse, gain):
    scaled = grad * gain
    return inverse * scaled - rows * inverse**3 * jnp.mean(scaled * rows, axis=-1, keepdims=True)


def halves_of(rows):
    count, width = rows.shape
    return rows.reshape(count, 2, width // 2).transpose(1, 0, 2)


def whole(pair):
    return pair.reshape(pair.shape[0] * pair.shape[1], pair.shape[2])


def per_device(
    tokens,
    seq_lengths,
    attn_gain,
    w_query,
    key_weight,
    value_weight,
    w_out,
    mlp_gain,
    w_gate,
    w_up,
    w_down,
    cotangent,
):
    lengths = seq_lengths[0]
    rep = lax.axis_index("rep")
    x, line = rep // 16, rep % 16
    inside = jnp.arange(128, dtype=jnp.int32)
    chunk = jnp.arange(4, dtype=jnp.int32)[:, None] * 16 + line
    rows_all = jnp.where(
        inside[None, :] < HALF,
        chunk * 128 + inside[None, :],
        (127 - 2 * chunk) * HALF + inside[None, :] - HALF,
    )
    starts = sequence_starts(lengths, rows_all)
    position = jnp.where(
        inside < HALF, rep * 128 + inside, (127 - 2 * rep) * HALF + inside - HALF
    ) - sequence_starts(
        lengths,
        jnp.where(inside < HALF, rep * 128 + inside, (127 - 2 * rep) * HALF + inside - HALF),
    )
    tables = rope_tables(position)
    gains = jnp.pad(jnp.concatenate([attn_gain, mlp_gain]), ((0, 12), (0, 96)))
    tokens, cotangent, gains, *first = start(
        tokens, cotangent, gains, (w_query, key_weight, value_weight)
    )
    gains = jnp.concatenate([gains[0, :4, :288], gains[1, :4, :288]], axis=1).astype(jnp.float32)
    projections = [[whole(item) for item in first], None]
    later = [None, None]

    hidden = tokens.astype(jnp.float32)
    kept = []
    for layer in range(DECODER_LAYERS):
        wq, wk, wv = projections[layer]
        inv_one = inverse_rms(hidden)
        normed = (hidden * inv_one * gains[layer]).astype(jnp.bfloat16)
        queries = rope(dot(normed, wq), tables, 1.0).astype(jnp.bfloat16) * 0.125
        keys = rope(dot(normed, wk), tables, 1.0).astype(jnp.bfloat16)
        values = dot(normed, wv).astype(jnp.bfloat16)
        joined = jnp.concatenate(
            [keys.reshape(128, 3, 64), values.reshape(128, 3, 64)], axis=-1
        ).reshape(128, 384)
        weights = [w_out, w_gate, w_up, w_down]
        layers = [layer] * 4
        if layer == 0:
            weights += [w_query, key_weight, value_weight]
            layers += [1] * 3
        queries_all, even, odd, *got = gather(
            queries, joined[:HALF], joined[HALF:], weights, layers, 1 + layer
        )
        got = [whole(item) for item in got]
        later[layer] = got[:4]
        if layer == 0:
            projections[1] = got[4:]
        wo, wg, wu, wd = later[layer]
        partial, logs = attend(queries_all, even, odd, starts)
        partial, logs = exchange_partials(partial, logs, 3 + layer)
        largest = jnp.max(logs, axis=0)
        shares = jnp.exp(logs - largest)
        total = jnp.sum(shares, axis=0)
        lse = largest + jnp.log(total)
        shares = (shares / total)[:, :QUERY_HEADS, None, :]
        outcome = jnp.sum(
            shares * partial.reshape(4, QUERY_HEADS, HEAD_SIZE, 128).astype(jnp.float32), axis=0
        )
        attended = outcome.reshape(MODEL_WIDTH, 128).astype(jnp.bfloat16).T
        middle = hidden + dot(attended, wo)
        inv_two = inverse_rms(middle)
        normed_two = (middle * inv_two * gains[2 + layer]).astype(jnp.bfloat16)
        gate = dot(normed_two, wg)
        up = dot(normed_two, wu)
        inner = (jax.nn.silu(gate) * up).astype(jnp.bfloat16)
        kept.append(
            (
                hidden,
                inv_one,
                normed,
                queries_all,
                even,
                odd,
                lse,
                outcome,
                attended,
                middle,
                inv_two,
                normed_two,
                gate,
                up,
                inner,
            )
        )
        hidden = middle + dot(inner, wd)
    activations = hidden.astype(jnp.bfloat16)

    grad = cotangent.astype(jnp.float32)
    collected = [None, None]
    for layer in (1, 0):
        (
            hidden,
            inv_one,
            normed,
            queries_all,
            even,
            odd,
            lse,
            outcome,
            attended,
            middle,
            inv_two,
            normed_two,
            gate,
            up,
            inner,
        ) = kept[layer]
        wq, wk, wv = projections[layer]
        wo, wg, wu, wd = later[layer]
        branch = grad.astype(jnp.bfloat16)
        grad_inner = dot_t(branch, wd)
        sigma = jax.nn.sigmoid(gate)
        grad_gate = (grad_inner * up * sigma * (1.0 + gate * (1.0 - sigma))).astype(jnp.bfloat16)
        grad_up = (grad_inner * gate * sigma).astype(jnp.bfloat16)
        grad_normed_two = dot_t(grad_gate, wg) + dot_t(grad_up, wu)
        grad_mlp_gain = jnp.sum(middle * inv_two * grad_normed_two, axis=0)
        grad_middle = grad + norm_back(grad_normed_two, middle, inv_two, gains[2 + layer])
        attn_branch = grad_middle.astype(jnp.bfloat16)
        grad_attended = dot_t(attn_branch, wo).astype(jnp.bfloat16)
        delta = jnp.sum(
            grad_attended.astype(jnp.float32).T.reshape(QUERY_HEADS, HEAD_SIZE, 128) * outcome,
            axis=1,
        )
        stats = jnp.stack([lse, jnp.pad(delta, ((0, 7), (0, 0)))])
        grads_all, stats_all, *swapped = back_gather(
            grad_attended,
            stats,
            [halves_of(item) for item in (normed, attended, normed_two, inner)],
            [branch, grad_gate, grad_up, attn_branch],
            5 + layer,
        )
        dq, dkv = attend_back(queries_all, even, odd, grads_all, stats_all, starts)
        dq, dkv = back_sum(dq, dkv, 7 + layer)
        dkv = dkv.reshape(128, 3, 128)
        grad_qp = rope(dq.T, tables, -1.0).astype(jnp.bfloat16)
        grad_kp = rope(dkv[:, :, :64].reshape(128, 192), tables, -1.0).astype(jnp.bfloat16)
        grad_vp = dkv[:, :, 64:].reshape(128, 192).astype(jnp.bfloat16)
        grad_normed = dot_t(grad_qp, wq) + dot_t(grad_kp, wk) + dot_t(grad_vp, wv)
        grad_attn_gain = jnp.sum(hidden * inv_one * grad_normed, axis=0)
        grad = grad_middle + norm_back(grad_normed, hidden, inv_one, gains[layer])
        gain_grads = jnp.pad(
            jnp.stack([grad_attn_gain, grad_mlp_gain]).reshape(2, 2, 288).transpose(1, 0, 2),
            ((0, 0), (0, 14), (0, 96)),
        )
        grad_qkv, gain_grads = pair_exchange(
            jnp.concatenate([grad_qp, grad_kp, grad_vp], axis=1), gain_grads, 9 + layer
        )
        summed = weight_grads(*swapped, grad_qkv, gain_grads)
        collected[layer] = reduce_grads(summed, 11 + layer)

    activations, grad = finish(activations, grad, 13)
    both = [item.astype(jnp.float32) for item in collected]

    def stacked(pick):
        return jnp.stack([pick(item) for item in both])

    return (
        activations,
        grad,
        stacked(lambda g: g[1152, :288]),
        stacked(lambda g: g[0:288, 0:576]),
        stacked(lambda g: g[0:288, 576:768]),
        stacked(lambda g: g[0:288, 768:960]),
        stacked(lambda g: g[0:288, 960:1536]),
        stacked(lambda g: g[1153, :288]),
        stacked(lambda g: g[288:576]),
        stacked(lambda g: g[576:864]),
        stacked(lambda g: jnp.concatenate([g[864:1152, :768], g[864:1152, 768:]], axis=0).T),
    )


def solution(mesh):
    rows = P(("shard", "rep"), None)
    gain, weight = P(None, "shard"), P(None, "shard", None)
    return jax.shard_map(
        per_device,
        mesh=mesh,
        in_specs=(
            rows,
            P("shard", None),
            gain,
            weight,
            weight,
            weight,
            weight,
            gain,
            weight,
            weight,
            weight,
            rows,
        ),
        out_specs=(
            rows,
            rows,
            gain,
            weight,
            weight,
            weight,
            weight,
            gain,
            weight,
            weight,
            weight,
        ),
        check_vma=False,
    )
```

time: 1500 us -> 787 us (0.52)
  waiting for transfers between devices: 848 us -> 0 us
  Pallas kernels: 0 us -> 667 us
  matrix products: 287 us -> 25.9 us
  blocking collectives: 181 us -> 0 us
  other arithmetic: 133 us -> 40.7 us
  local copies, waits for them, and re-layouts: 23 us -> 45.7 us
  between operations: 18.6 us -> 1.97 us
    pallas_call x0 -> x20, Pallas kernels: none -> 667 us  [the longest x14 583 us: comm_call(): pl.pallas_call(kernel, out_shape=outs, in_specs=in_specs, out_specs=out_s...]
    reduce_scatter x16 -> x0, waiting for transfers between devices: 524 us -> none  [the longest x2 450 us: backward_layer(): lax.psum_scatter(buffer, 'rep', scatter_dimension=0, tiled=True)]
    dot_general x56 -> x28, matrix products: 287 us -> 25.9 us  [the longest x14 14.2 us: dot_t(): jnp.einsum('ta,ba->tb', left, right, preferred_element_type=jnp.float32)]
    all_gather x10 -> x0, waiting for transfers between devices: 256 us -> none  [the longest x2 149 us: forward_layer(): value_slice = lax.all_gather(values_now, 'rep', axis=0, tiled=True)]
    psum x1 -> x0, blocking collectives: 156 us -> none  [per_device(): lax.psum((owned[0], owned[1], owned[2], owned[3], owned[4], owned[5], own...]
    psum x1 -> x0, waiting for transfers between devices: 65.7 us -> none  [per_device(): lax.psum((owned[0], owned[1], owned[2], owned[3], owned[4], owned[5], own...]
    another operation x35 -> x18, other arithmetic: 46.7 us -> 14 us  [the longest x11 11.8 us: stacked(): return jnp.stack([pick(item) for item in both])]
    reduce_sum x11, other arithmetic: 37.6 us -> 5.99 us  [the longest x2 2.43 us: per_device(): jnp.sum(shares * partial.reshape(4, QUERY_HEADS, HEAD_SIZE, 128).astype(j...]
  transfers between devices with their start and end apart: 27 -> 0, of which waited for: 13 -> 0; matrix products, arithmetic and copies ran while one was open for 21% -> 0% of each run, Pallas kernels for 0% -> 0%
where the time goes in v1:
time: 787 us; the launch traced here: 781 us
  Pallas kernels  667 us (85%)
  local copies, waits for them, and re-layouts  45.7 us (6%)
  other arithmetic  40.7 us (5%)
  matrix products  25.9 us (3%)
    pallas_call x14, Pallas kernels, comm_call(): pl.pallas_call(kernel, out_shape=outs, in_specs=in_specs, out_specs=out_s...  583 us
    pallas_call x2, Pallas kernels, attend_back(): pl.pallas_call(attend_back_kernel, out_shape=[shape_of((4, MODEL_WIDTH, 1...  42.3 us
    pallas_call x2, Pallas kernels, attend(): pl.pallas_call(attend_kernel, out_shape=[shape_of((4, MODEL_WIDTH, 128),...  31.8 us
    unnamed x109, local copies, waits for them, and re-layouts  19.9 us

profile of v1, /device:TPU:1, one launch (start us, length us, event | category | flops | bytes accessed | tf_op | source)
XLA Modules:
  0.0 781.4 jit_solution(155527406543386742)
XLA Ops:
  3.2 1.3 fusion.25.refs_2_
  4.6 1.7 copy.261.refs_0_
  6.4 1.7 copy.262.refs_1_
  8.1 35.9 %start_rows.1 = (bf16[128,576]{1,0:T(8,128)(2,1)}, bf16[128,576]{1,0:T(8,128)(2,1)}, bf16[2,16,384]{2,1,0:T(8,128)(2,1)}, bf16[2,288,576]{2,1,0:T(8,128)(2,1)}, ...) custom-call(bf16[128,576]{1,0:T(8,128)(2,1)} %copy.261.refs_0_, bf16[128,576]{1,0:T(8,128)(2,1)} %copy.262.refs_1_, ...), custom_call_target="tpu_custom_call" | custom-call | tf_op jit(solution)/shard_map/start_rows/pallas_call | solution.py:91
  44.8 1.0 fusion.7
  47.0 1.0 fusion.5
  48.0 1.3 convolution_convert_fusion.3
  53.8 4.4 copy.271.refs_6_
  58.2 125.2 %gather_qkv_1.1 = (bf16[4,128,576]{2,1,0:T(8,128)(2,1)}, bf16[4,4,64,384]{3,2,1,0:T(8,128)(2,1)}, bf16[4,4,64,384]{3,2,1,0:T(8,128)(2,1)}, bf16[2,288,576]{2,1,0...) custom-call(bf16[128,576]{1,0:T(8,128)(2,1)} %copy.270.refs_0_, ...), custom_call_target="tpu_custom_call" | custom-call | tf_op jit(solution)/shard_map/gather_qkv_1/pallas_call | solution.py:91
  183.3 1.8 copy.276
  185.2 15.8 %attend.2 = (bf16[4,576,128]{2,1,0:T(8,128)(2,1)}, f32[4,16,128]{2,1,0:T(8,128)}) custom-call(bf16[4,128,576]{2,1,0:T(8,128)(2,1)} %get-tuple-element.81.q_ref, bf16[1024,384]{1,0:T(8,128)(2,1)} %bitcast.233, bf16[1024,384]{1,0:T(8,128)(2,1)} %bitcast.235, s32[4,128]{1,0:T(4,128)} %select_reduce_fusion.starts_ref), custom_call_target="tpu_custom_call" | custom-call | tf_op jit(solution)/shard_map/attend/pallas_call | solution.py:315
  201.0 9.8 %swap_partials_3.1 = (bf16[4,576,128]{2,1,0:T(8,128)(2,1)}, f32[4,16,128]{2,1,0:T(8,128)}) custom-call(bf16[4,576,128]{2,1,0:T(8,128)(2,1)} %get-tuple-element.84.o_ref, f32[4,16,128]{2,1,0:T(8,128)} %get-tuple-element.85.lse_ref), custom_call_target="tpu_custom_call" | custom-call | tf_op jit(solution)/shard_map/swap_partials_3/pallas_call | solution.py:91
  212.9 1.2 fusion.1
  214.2 0.9 copy.303
  218.5 1.5 copy.274
  220.4 1.0 copy-done.14
  221.4 1.4 multiply_convert_fusion.5
  226.3 1.3 convolution_convert_fusion.2
  229.6 1.2 pad_maximum_fusion.10
  232.9 106.9 %gather_qkv_2.1 = (bf16[4,128,576]{2,1,0:T(8,128)(2,1)}, bf16[4,4,64,384]{3,2,1,0:T(8,128)(2,1)}, bf16[4,4,64,384]{3,2,1,0:T(8,128)(2,1)}, bf16[2,288,576]{2,1,0...) custom-call(bf16[128,576]{1,0:T(8,128)(2,1)} %copy.281.refs_0_, ...), custom_call_target="tpu_custom_call" | custom-call | tf_op jit(solution)/shard_map/gather_qkv_2/pallas_call | solution.py:91
  339.8 16.0 %attend.3 = (bf16[4,576,128]{2,1,0:T(8,128)(2,1)}, f32[4,16,128]{2,1,0:T(8,128)}) custom-call(bf16[4,128,576]{2,1,0:T(8,128)(2,1)} %get-tuple-element.95.q_ref, bf16[1024,384]{1,0:T(8,128)(2,1)} %bitcast.237, bf16[1024,384]{1,0:T(8,128)(2,1)} %bitcast.239, s32[4,128]{1,0:T(4,128)} %select_reduce_fusion.starts_ref), custom_call_target="tpu_custom_call" | custom-call | tf_op jit(solution)/shard_map/attend/pallas_call | solution.py:315
  355.8 9.2 %swap_partials_4.1 = (bf16[4,576,128]{2,1,0:T(8,128)(2,1)}, f32[4,16,128]{2,1,0:T(8,128)}) custom-call(bf16[4,576,128]{2,1,0:T(8,128)(2,1)} %get-tuple-element.98.o_ref, f32[4,16,128]{2,1,0:T(8,128)} %get-tuple-element.99.lse_ref), custom_call_target="tpu_custom_call" | custom-call | tf_op jit(solution)/shard_map/swap_partials_4/pallas_call | solution.py:91
  366.6 1.2 fusion
  367.9 0.9 copy.288
  369.6 1.5 multiply_reduce_fusion.6
  372.2 2.1 fusion.40
  374.8 1.1 copy-done.13
  376.8 1.1 fusion.2.acts
  379.4 1.5 multiply_reduce_fusion
  382.4 1.8 fusion.29
  384.2 1.1 bitcast_multiply_fusion.3
  386.1 58.2 %gather_grads_6.1 = (bf16[4,128,576]{2,1,0:T(8,128)(2,1)}, f32[4,2,16,128]{3,2,1,0:T(8,128)}, bf16[2,128,288]{2,1,0:T(8,128)(2,1)}, bf16[2,128,288]{2,1,0:T(8,12...) custom-call(bf16[128,576]{1,0:T(8,128)(2,1)} %get-tuple-element.286., ...), custom_call_target="tpu_custom_call" | custom-call | tf_op jit(solution)/shard_map/gather_grads_6/pallas_call | solution.py:91
  444.3 21.1 %attend_back.2 = (bf16[4,576,128]{2,1,0:T(8,128)(2,1)}, bf16[2,1024,384]{2,1,0:T(8,128)(2,1)}) custom-call(bf16[4,128,576]{2,1,0:T(8,128)(2,1)} %get-tuple-element.95.q_ref, bf16[1024,384]{1,0:T(8,128)(2,1)} %bitcast.238, bf16[1024,384]{1,0:T(8,128)(2,1)} %bitcast.240, bf16[4,128,576]{2,1,0:T(8,128)(2,1)} %get-tuple-element.107.do_ref, ...), custom_call_target="tpu_custom_call" | custom-call | tf_op jit(solution)/shard_map/attend_back/pallas_call | solution.py:469
  465.3 18.2 %sum_dqkv_8.1 = (f32[576,128]{1,0:T(8,128)}, f32[128,384]{1,0:T(8,128)}) custom-call(bf16[4,576,128]{2,1,0:T(8,128)(2,1)} %get-tuple-element.109.dq_ref, bf16[2,4,4,64,384]{4,3,2,1,0:T(8,128)(2,1)} %bitcast.259), custom_call_target="tpu_custom_call" | custom-call | tf_op jit(solution)/shard_map/sum_dqkv_8/pallas_call | solution.py:91
  483.5 1.1 multiply_subtract_fusion.1
  486.1 1.2 convolution_add_fusion.4
  487.3 1.3 multiply_reduce_fusion.1
  488.7 1.8 fusion.28
  490.6 2.8 multiply_convert_fusion
  494.2 1.0 copy-done.15
  495.2 1.5 multiply_reduce_fusion.2
  496.8 1.1 fusion.27
  498.0 1.1 bitcast_multiply_fusion.2
  501.6 12.0 %swap_cores_10.1 = (bf16[2,128,960]{2,1,0:T(8,128)(2,1)}, f32[2,16,384]{2,1,0:T(8,128)}) custom-call(bf16[128,960]{1,0:T(8,128)(2,1)} %pad_maximum_fusion.8.qkv, f32[2,16,384]{2,1,0:T(8,128)} %pad.22.gains), custom_call_target="tpu_custom_call" | custom-call | tf_op jit(solution)/shard_map/swap_cores_10/pallas_call | solution.py:91
  513.6 5.1 weight_grads.3.g_ref
  518.7 52.0 %sum_weight_grads_12.1 = bf16[1216,1536]{1,0:T(8,128)(2,1)} custom-call(bf16[1216,1536]{1,0:T(8,128)(2,1)} %weight_grads.3.g_ref), custom_call_target="tpu_custom_call" | custom-call | tf_op jit(solution)/shard_map/sum_weight_grads_12/pallas_call | solution.py:91
  571.5 58.5 %gather_grads_5.1 = (bf16[4,128,576]{2,1,0:T(8,128)(2,1)}, f32[4,2,16,128]{3,2,1,0:T(8,128)}, bf16[2,128,288]{2,1,0:T(8,128)(2,1)}, bf16[2,128,288]{2,1,0:T(8,12...) custom-call(bf16[128,576]{1,0:T(8,128)(2,1)} %get-tuple-element.290., ...), custom_call_target="tpu_custom_call" | custom-call | tf_op jit(solution)/shard_map/gather_grads_5/pallas_call | solution.py:91
  630.0 21.2 %attend_back.3 = (bf16[4,576,128]{2,1,0:T(8,128)(2,1)}, bf16[2,1024,384]{2,1,0:T(8,128)(2,1)}) custom-call(bf16[4,128,576]{2,1,0:T(8,128)(2,1)} %get-tuple-element.81.q_ref, bf16[1024,384]{1,0:T(8,128)(2,1)} %bitcast.234, bf16[1024,384]{1,0:T(8,128)(2,1)} %bitcast.236, bf16[4,128,576]{2,1,0:T(8,128)(2,1)} %get-tuple-element.113.do_ref, ...), custom_call_target="tpu_custom_call" | custom-call | tf_op jit(solution)/shard_map/attend_back/pallas_call | solution.py:469
  651.2 18.1 %sum_dqkv_7.1 = (f32[576,128]{1,0:T(8,128)}, f32[128,384]{1,0:T(8,128)}) custom-call(bf16[4,576,128]{2,1,0:T(8,128)(2,1)} %get-tuple-element.115.dq_ref, bf16[2,4,4,64,384]{4,3,2,1,0:T(8,128)(2,1)} %bitcast.258), custom_call_target="tpu_custom_call" | custom-call | tf_op jit(solution)/shard_map/sum_dqkv_7/pallas_call | solution.py:91
  669.3 1.1 multiply_subtract_fusion
  672.9 13.1 %return_rows.1 = (bf16[128,576]{1,0:T(8,128)(2,1)}, f32[128,576]{1,0:T(8,128)}) custom-call(bf16[128,576]{1,0:T(8,128)(2,1)} %fusion.2.acts, f32[128,576]{1,0:T(8,128)} %fusion.10.grads), custom_call_target="tpu_custom_call" | custom-call | tf_op jit(solution)/shard_map/return_rows/pallas_call | solution.py:91
  686.0 1.7 copy.321
  689.3 11.3 %swap_cores_9.1 = (bf16[2,128,960]{2,1,0:T(8,128)(2,1)}, f32[2,16,384]{2,1,0:T(8,128)}) custom-call(bf16[128,960]{1,0:T(8,128)(2,1)} %pad_maximum_fusion.7.qkv, f32[2,16,384]{2,1,0:T(8,128)} %pad.21.gains), custom_call_target="tpu_custom_call" | custom-call | tf_op jit(solution)/shard_map/swap_cores_9/pallas_call | solution.py:91
  700.7 5.1 weight_grads.2.g_ref
  705.7 54.4 %sum_weight_grads_11.1 = bf16[1216,1536]{1,0:T(8,128)(2,1)} custom-call(bf16[1216,1536]{1,0:T(8,128)(2,1)} %weight_grads.2.g_ref), custom_call_target="tpu_custom_call" | custom-call | tf_op jit(solution)/shard_map/sum_weight_grads_11/pallas_call | solution.py:91
  763.0 1.4 fusion.32
  765.5 2.0 pad_maximum_fusion.2
  767.6 1.0 convert_element_type.252
  769.3 1.8 copy-done.1
  771.1 1.0 convert_element_type.251
  774.5 2.1 pad_maximum_fusion.1
  776.6 1.2 pad_maximum_fusion.4
  777.8 1.2 pad_maximum_fusion.3
  779.0 2.1 pad_maximum_fusion
  (235 shorter events, 47.6 us)
Async XLA Ops:
  44.0 6.4 copy-start.30
  46.4 0.6 copy-start.42
  49.3 2.9 copy-start.6
  201.0 14.9 %copy-start.5 = (bf16[128,576]{1,0:T(8,128)(2,1)S(1)}, bf16[128,576]{1,0:T(8,128)(2,1)}, u32[]{:S(2)}) copy-start(bf16[128,576]{1,0:T(8,128)(2,1)} %get-tuple-element.76) | copy-start | bytes 442372
  201.0 14.9 %copy-start.8 = (bf16[2,288,576]{2,1,0:T(8,128)(2,1)S(1)}, bf16[2,288,576]{2,1,0:T(8,128)(2,1)}, u32[]{:S(2)}) copy-start(bf16[2,288,576]{2,1,0:T(8,128)(2,1)} %get-tuple-element.88) | copy-start | bytes 1990660
  215.9 4.0 copy-start.2
  216.9 0.5 copy-start.44
  219.9 1.5 copy-start.14
  221.4 1.4 copy-start.33
  221.4 2.1 copy-start.12
  222.8 2.3 copy-start.16
  223.5 1.6 copy-start.32
  224.6 0.8 copy-start.46
  225.4 6.7 copy-start.17
  372.2 2.1 copy-start.3
  374.3 1.5 copy-start.13
  374.3 1.5 copy-start.35
  376.8 1.9 copy-start.19
  376.8 1.9 copy-start.20
  376.8 1.9 copy-start.23
  377.9 1.5 copy-start.4
  379.4 2.2 copy-start.21
  381.6 2.6 copy-start.11
  381.6 2.6 copy-start.27
  384.2 1.9 copy-start.25
  465.3 19.3 %copy-start.10 = (bf16[2,288,576]{2,1,0:T(8,128)(2,1)S(1)}, bf16[2,288,576]{2,1,0:T(8,128)(2,1)}, u32[]{:S(2)}) copy-start(bf16[2,288,576]{2,1,0:T(8,128)(2,1)} %get-tuple-element.92) | copy-start | bytes 1990660
  483.5 2.4 copy-start.38
  484.6 2.7 copy-start.47
  485.0 3.7 copy-start.41
  485.1 3.7 copy-start.50
  490.6 2.9 copy-start.34
  493.5 3.3 copy-start.18
  493.5 3.3 copy-start.22
  493.5 1.8 copy-start.15
  493.5 1.8 copy-start.45
  494.2 2.6 copy-start.28
  494.2 2.6 copy-start.49
  495.2 2.8 copy-start.9
  495.2 2.8 copy-start.26
  496.8 2.4 copy-start.40
  498.0 3.6 copy-start.24
  498.0 2.1 copy-start.36
  651.2 19.3 %copy-start.7 = (bf16[2,288,576]{2,1,0:T(8,128)(2,1)S(1)}, bf16[2,288,576]{2,1,0:T(8,128)(2,1)}, u32[]{:S(2)}) copy-start(bf16[2,288,576]{2,1,0:T(8,128)(2,1)} %get-tuple-element.78) | copy-start | bytes 1990660
  669.3 1.7 copy-start.39
  669.3 1.9 copy-start.31
  670.4 1.1 copy-start.29
  670.4 1.1 copy-start.43
  670.9 1.1 copy-start.48
  705.7 56.4 %copy-start.37 = (f32[128,576]{1,0:T(8,128)S(1)}, f32[128,576]{1,0:T(8,128)}, u32[]{:S(2)}) copy-start(f32[128,576]{1,0:T(8,128)} %get-tuple-element.186) | copy-start | bytes 884740
  763.0 2.3 copy-start
  769.0 2.1 copy-start.1
